TPU v7x, 256 devices: a whole 4x4x8 slice. The times are simulated.
256 devices in a mesh: tm: 16 (over z, core), space: 16 (over y, x).
Axes of the slice: x: 4, y: 4, z: 8, core: 2. Of those that a mesh axis runs over, the one named last changes fastest.
Arguments:
- coarse_guess: float32 [32, 512, 2048], P('tm', 'space'), may hold values from -2.5 to 2.5
- initial: float32 [512, 2048], P('space'), may hold values from -2.5 to 2.5
- diffusion: float32 [512, 2048], P('space'), may hold values from 0.002 to 0.008
- velocity: float32 [2, 512, 2048], P(None, 'space'), may hold values from -0.04 to 0.04
- reaction: float32 [512, 2048], P('space'), may hold values from 0.002 to 0.006
- source: float32 [512, 2048], P('space'), may hold values from -0.2 to 0.2
Outputs:
- corrected: float32 [32, 512, 2048], P('tm', 'space')
All inputs are finite; a program needn't handle non-finite values.
Results may differ from a plain program's by a relative error of at most 0.00002.
Values sent between devices are 32-bit elements; how exact they have to be, the bound alone decides.
A program may use at most 128 MiB of HBM per device.

v0:
```python
import jax
import jax.numpy as jnp
from jax import lax
from jax.sharding import PartitionSpec as P

COARSEN = 8


def with_halo(array, sides, width):
    for axis, dim in sides:
        peers, length = (lax.axis_size(axis), array.shape[dim])
        up = [(i, (i + 1) % peers) for i in range(peers - 1)]
        down = [(j, i) for i, j in up]
        last = lax.slice_in_dim(array, length - width, length, axis=dim)
        initial = lax.slice_in_dim(array, 0, width, axis=dim)
        before = lax.ppermute(last, axis, up)
        after = lax.ppermute(initial, axis, down)
        array = jnp.concatenate([before, array, after], axis=dim)
    return array


def shifted(block, axis, distance):
    devices = range(lax.axis_size(axis))
    route = [(i - distance, i) for i in devices if i - distance in devices]
    return lax.ppermute(block, axis, route)


def advance(padded, coefficients, factor):
    diffusion = coefficients[0]
    vel_row = coefficients[1]
    vel_col = coefficients[2]
    reaction = coefficients[3]
    source = coefficients[4]
    centre = padded[..., 1:-1, :]
    upper_row = padded[..., :-2, :]
    lower_row = padded[..., 2:, :]
    left_cell = jnp.roll(centre, 1, axis=-1)
    right_cell = jnp.roll(centre, -1, axis=-1)
    laplace = upper_row + lower_row + left_cell + right_cell - 4.0 * centre
    transport = jnp.maximum(vel_row, 0.0) * (centre - upper_row) + jnp.minimum(vel_row, 0.0) * (
        lower_row - centre
    )
    transport = (
        transport
        + jnp.maximum(vel_col, 0.0) * (centre - left_cell)
        + jnp.minimum(vel_col, 0.0) * (right_cell - centre)
    )
    change = (
        diffusion * laplace + reaction * (centre - centre * centre * centre) + source - transport
    )
    return centre + factor * change


def fine_halo(field, coefficients):
    padded = with_halo(field, (("space", 1),), 1)
    return (padded, advance(padded, coefficients, 1.0))


def propagate(starts, coefficients):
    first_padded, field = fine_halo(starts, coefficients)
    for repeat in range(COARSEN - 1):
        unused, field = fine_halo(field, coefficients)
    return (field, first_padded)


def start_values(values, initial):
    last_value = shifted(values[-1], "tm", 1)
    before = jnp.where(lax.axis_index("tm") == 0, initial, last_value)
    return jnp.concatenate([before[None], values[:-1]], axis=0)


def coarse_step(field, forcing_term, coefficients):
    padded = with_halo(field, (("space", 0),), 1)
    return advance(padded, coefficients, float(COARSEN)) + forcing_term


def shards(coarse_guess, initial, diffusion, velocity, reaction, source):
    coefficients = jnp.stack([diffusion, velocity[0], velocity[1], reaction, source])
    starts = start_values(coarse_guess, initial)
    relaxed, unused = propagate(starts, coefficients)
    again = start_values(relaxed, initial)
    fine_end, first_padded = propagate(again, coefficients)
    forcing = fine_end - advance(first_padded, coefficients, float(COARSEN))
    count_local = forcing.shape[0]
    tm_first = lax.axis_index("tm") == 0

    def run_chain(incoming):
        fields = []
        field = incoming
        for index_c in range(count_local):
            field = coarse_step(field, forcing[index_c], coefficients)
            fields.append(field)
        return jnp.stack(fields)

    def one_round(round_index, incoming):
        values = run_chain(incoming)
        sent = shifted(values[-1], "tm", 1)
        return jnp.where(tm_first, initial, sent)

    incoming = lax.fori_loop(0, lax.axis_size("tm") - 1, one_round, initial)
    corrected = run_chain(incoming)
    return corrected


def solution(mesh):
    return jax.shard_map(
        shards,
        mesh=mesh,
        in_specs=(
            P("tm", "space", None),
            P("space", None),
            P("space", None),
            P(None, "space", None),
            P("space", None),
            P("space", None),
        ),
        out_specs=P("tm", "space", None),
        check_vma=False,
    )
```

profile of v0, /device:TPU:142, one launch (start us, length us, event | category | flops | bytes accessed | tf_op | source)
XLA Modules:
  0.0 649.5 jit_solution(17567902909864706334)
XLA Ops:
  3.2 6.8 %collective-permute-done.5 = f32[32,2048]{1,0:T(8,128)S(1)} collective-permute-done((f32[32,2048]{1,0:T(8,128)S(1)}, f32[32,2048]{1,0:T(8,128)S(1)}, u32[]{:S(2)}, u32[]{:S(2)}) %collective-permute-start.5) | collective-permute-done | bytes 262176 | tf_op jit(solution)/shard_map/ppermute | solution.py:25
  97.8 6.9 %collective-permute-done.22 = f32[32,2048]{1,0:T(8,128)S(1)} collective-permute-done((f32[32,2048]{1,0:T(8,128)S(1)}, f32[32,2048]{1,0:T(8,128)S(1)}, u32[]{:S(2)}, u32[]{:S(2)}) %collective-permute-start.22) | collective-permute-done | bytes 262176 | tf_op jit(solution)/shard_map/ppermute | solution.py:25
  189.1 435.0 %while.10 = (s32[]{:T(128)}, f32[32,2048]{1,0:T(8,128)S(1)}, pred[]{:T(512)}, f32[32,2048]{1,0:T(8,128)S(1)}, f32[32,2048]{1,0:T(8,128)S(1)}, /*index=5*/f32[32,...) while((s32[]{:T(128)}, f32[32,2048]{1,0:T(8,128)S(1)}, ...), condition=%wide.region_1.2_spmd, body=%wide.region_0.1_spmd.sunk | while | flops 4653058 | bytes 9404726 | solution.py:100
  191.1 6.0 collective-permute-start.1
  200.9 6.3 collective-permute-start.3
  210.9 7.0 %collective-permute-done.4 = f32[32,2048]{1,0:T(8,128)S(1)} collective-permute-done((f32[32,2048]{1,0:T(8,128)S(1)}, f32[32,2048]{1,0:T(8,128)S(1)}, u32[]{:S(2)}, u32[]{:S(2)}) %collective-permute-start.4) | collective-permute-done | bytes 262176 | tf_op jit(solution)/shard_map/while/body/eval_jaxpr/ppermute | solution.py:25
  220.5 5.6 collective-permute-start.1
  230.6 5.6 collective-permute-start.3
  239.9 7.0 %collective-permute-done.4 = f32[32,2048]{1,0:T(8,128)S(1)} collective-permute-done((f32[32,2048]{1,0:T(8,128)S(1)}, f32[32,2048]{1,0:T(8,128)S(1)}, u32[]{:S(2)}, u32[]{:S(2)}) %collective-permute-start.4) | collective-permute-done | bytes 262176 | tf_op jit(solution)/shard_map/while/body/eval_jaxpr/ppermute | solution.py:25
  259.6 5.6 collective-permute-start.3
  268.9 7.0 %collective-permute-done.4 = f32[32,2048]{1,0:T(8,128)S(1)} collective-permute-done((f32[32,2048]{1,0:T(8,128)S(1)}, f32[32,2048]{1,0:T(8,128)S(1)}, u32[]{:S(2)}, u32[]{:S(2)}) %collective-permute-start.4) | collective-permute-done | bytes 262176 | tf_op jit(solution)/shard_map/while/body/eval_jaxpr/ppermute | solution.py:25
  297.9 7.0 %collective-permute-done.4 = f32[32,2048]{1,0:T(8,128)S(1)} collective-permute-done((f32[32,2048]{1,0:T(8,128)S(1)}, f32[32,2048]{1,0:T(8,128)S(1)}, u32[]{:S(2)}, u32[]{:S(2)}) %collective-permute-start.4) | collective-permute-done | bytes 262176 | tf_op jit(solution)/shard_map/while/body/eval_jaxpr/ppermute | solution.py:25
  326.9 7.0 %collective-permute-done.4 = f32[32,2048]{1,0:T(8,128)S(1)} collective-permute-done((f32[32,2048]{1,0:T(8,128)S(1)}, f32[32,2048]{1,0:T(8,128)S(1)}, u32[]{:S(2)}, u32[]{:S(2)}) %collective-permute-start.4) | collective-permute-done | bytes 262176 | tf_op jit(solution)/shard_map/while/body/eval_jaxpr/ppermute | solution.py:25
  355.9 7.0 %collective-permute-done.4 = f32[32,2048]{1,0:T(8,128)S(1)} collective-permute-done((f32[32,2048]{1,0:T(8,128)S(1)}, f32[32,2048]{1,0:T(8,128)S(1)}, u32[]{:S(2)}, u32[]{:S(2)}) %collective-permute-start.4) | collective-permute-done | bytes 262176 | tf_op jit(solution)/shard_map/while/body/eval_jaxpr/ppermute | solution.py:25
  385.0 7.0 %collective-permute-done.4 = f32[32,2048]{1,0:T(8,128)S(1)} collective-permute-done((f32[32,2048]{1,0:T(8,128)S(1)}, f32[32,2048]{1,0:T(8,128)S(1)}, u32[]{:S(2)}, u32[]{:S(2)}) %collective-permute-start.4) | collective-permute-done | bytes 262176 | tf_op jit(solution)/shard_map/while/body/eval_jaxpr/ppermute | solution.py:25
  414.0 7.0 %collective-permute-done.4 = f32[32,2048]{1,0:T(8,128)S(1)} collective-permute-done((f32[32,2048]{1,0:T(8,128)S(1)}, f32[32,2048]{1,0:T(8,128)S(1)}, u32[]{:S(2)}, u32[]{:S(2)}) %collective-permute-start.4) | collective-permute-done | bytes 262176 | tf_op jit(solution)/shard_map/while/body/eval_jaxpr/ppermute | solution.py:25
  443.0 7.0 %collective-permute-done.4 = f32[32,2048]{1,0:T(8,128)S(1)} collective-permute-done((f32[32,2048]{1,0:T(8,128)S(1)}, f32[32,2048]{1,0:T(8,128)S(1)}, u32[]{:S(2)}, u32[]{:S(2)}) %collective-permute-start.4) | collective-permute-done | bytes 262176 | tf_op jit(solution)/shard_map/while/body/eval_jaxpr/ppermute | solution.py:25
  472.0 7.0 %collective-permute-done.4 = f32[32,2048]{1,0:T(8,128)S(1)} collective-permute-done((f32[32,2048]{1,0:T(8,128)S(1)}, f32[32,2048]{1,0:T(8,128)S(1)}, u32[]{:S(2)}, u32[]{:S(2)}) %collective-permute-start.4) | collective-permute-done | bytes 262176 | tf_op jit(solution)/shard_map/while/body/eval_jaxpr/ppermute | solution.py:25
  501.0 7.0 %collective-permute-done.4 = f32[32,2048]{1,0:T(8,128)S(1)} collective-permute-done((f32[32,2048]{1,0:T(8,128)S(1)}, f32[32,2048]{1,0:T(8,128)S(1)}, u32[]{:S(2)}, u32[]{:S(2)}) %collective-permute-start.4) | collective-permute-done | bytes 262176 | tf_op jit(solution)/shard_map/while/body/eval_jaxpr/ppermute | solution.py:25
  530.0 7.0 %collective-permute-done.4 = f32[32,2048]{1,0:T(8,128)S(1)} collective-permute-done((f32[32,2048]{1,0:T(8,128)S(1)}, f32[32,2048]{1,0:T(8,128)S(1)}, u32[]{:S(2)}, u32[]{:S(2)}) %collective-permute-start.4) | collective-permute-done | bytes 262176 | tf_op jit(solution)/shard_map/while/body/eval_jaxpr/ppermute | solution.py:25
  559.0 7.0 %collective-permute-done.4 = f32[32,2048]{1,0:T(8,128)S(1)} collective-permute-done((f32[32,2048]{1,0:T(8,128)S(1)}, f32[32,2048]{1,0:T(8,128)S(1)}, u32[]{:S(2)}, u32[]{:S(2)}) %collective-permute-start.4) | collective-permute-done | bytes 262176 | tf_op jit(solution)/shard_map/while/body/eval_jaxpr/ppermute | solution.py:25
  588.1 7.0 %collective-permute-done.4 = f32[32,2048]{1,0:T(8,128)S(1)} collective-permute-done((f32[32,2048]{1,0:T(8,128)S(1)}, f32[32,2048]{1,0:T(8,128)S(1)}, u32[]{:S(2)}, u32[]{:S(2)}) %collective-permute-start.4) | collective-permute-done | bytes 262176 | tf_op jit(solution)/shard_map/while/body/eval_jaxpr/ppermute | solution.py:25
  617.1 7.0 %collective-permute-done.4 = f32[32,2048]{1,0:T(8,128)S(1)} collective-permute-done((f32[32,2048]{1,0:T(8,128)S(1)}, f32[32,2048]{1,0:T(8,128)S(1)}, u32[]{:S(2)}, u32[]{:S(2)}) %collective-permute-start.4) | collective-permute-done | bytes 262176 | tf_op jit(solution)/shard_map/while/body/eval_jaxpr/ppermute | solution.py:25
  624.3 6.3 collective-permute-start.39
  (427 shorter events, 493.6 us)
Async XLA Ops:
  1.1 8.9 %collective-permute-start.5 = (f32[32,2048]{1,0:T(8,128)S(1)}, f32[32,2048]{1,0:T(8,128)S(1)}, u32[]{:S(2)}, u32[]{:S(2)}) collective-permute-start(f32[32,2048]{1,0:T(8,128)S(1)} %get-tuple-element.196), channel_id=1, source_target_pairs={{0,16},{16,32},{32,48},{48,64},{64,80},{80,96},{96,112},{112,128},... | collective-permute-start | bytes 786440 | tf_op jit(solution)/shard_map/ppermute | solution.py:25
  95.9 8.9 %collective-permute-start.22 = (f32[32,2048]{1,0:T(8,128)S(1)}, f32[32,2048]{1,0:T(8,128)S(1)}, u32[]{:S(2)}, u32[]{:S(2)}) collective-permute-start(f32[32,2048]{1,0:T(8,128)S(1)} %get-tuple-element.140), channel_id=1, source_target_pairs={{0,16},{16,32},{32,48},{48,64},{64,80},{80,96},{96,112},{112,128},... | collective-permute-start | bytes 786440 | tf_op jit(solution)/shard_map/ppermute | solution.py:25
  208.9 8.9 %collective-permute-start.4 = (f32[32,2048]{1,0:T(8,128)S(1)}, f32[32,2048]{1,0:T(8,128)S(1)}, u32[]{:S(2)}, u32[]{:S(2)}) collective-permute-start(f32[32,2048]{1,0:T(8,128)S(1)} %fusion.408), channel_id=1, source_target_pairs={{0,16},{16,32},{32,48},{48,64},{64,80},{80,96},{96,112},{112,128},... | collective-permute-start | bytes 786440 | tf_op jit(solution)/shard_map/while/body/eval_jaxpr/ppermute | solution.py:25
  217.9 8.5 %collective-permute-start = (f32[1,2048]{1,0:T(1,128)S(1)}, f32[1,2048]{1,0:T(1,128)S(1)}, u32[]{:S(2)}, u32[]{:S(2)}) collective-permute-start(f32[1,2048]{1,0:T(1,128)S(1)} %get-tuple-element.283), channel_id=1, source_target_pairs={{1,0},{2,1},{3,2},{4,3},{5,4},{6,5},{7,6},{8,7},{9,8},{10,9},{11,1... | collective-permute-start | bytes 24584 | tf_op jit(solution)/shard_map/while/body/eval_jaxpr/ppermute | solution.py:17
  238.0 8.9 %collective-permute-start.4 = (f32[32,2048]{1,0:T(8,128)S(1)}, f32[32,2048]{1,0:T(8,128)S(1)}, u32[]{:S(2)}, u32[]{:S(2)}) collective-permute-start(f32[32,2048]{1,0:T(8,128)S(1)} %fusion.408), channel_id=1, source_target_pairs={{0,16},{16,32},{32,48},{48,64},{64,80},{80,96},{96,112},{112,128},... | collective-permute-start | bytes 786440 | tf_op jit(solution)/shard_map/while/body/eval_jaxpr/ppermute | solution.py:25
  267.0 8.9 %collective-permute-start.4 = (f32[32,2048]{1,0:T(8,128)S(1)}, f32[32,2048]{1,0:T(8,128)S(1)}, u32[]{:S(2)}, u32[]{:S(2)}) collective-permute-start(f32[32,2048]{1,0:T(8,128)S(1)} %fusion.408), channel_id=1, source_target_pairs={{0,16},{16,32},{32,48},{48,64},{64,80},{80,96},{96,112},{112,128},... | collective-permute-start | bytes 786440 | tf_op jit(solution)/shard_map/while/body/eval_jaxpr/ppermute | solution.py:25
  296.0 8.9 %collective-permute-start.4 = (f32[32,2048]{1,0:T(8,128)S(1)}, f32[32,2048]{1,0:T(8,128)S(1)}, u32[]{:S(2)}, u32[]{:S(2)}) collective-permute-start(f32[32,2048]{1,0:T(8,128)S(1)} %fusion.408), channel_id=1, source_target_pairs={{0,16},{16,32},{32,48},{48,64},{64,80},{80,96},{96,112},{112,128},... | collective-permute-start | bytes 786440 | tf_op jit(solution)/shard_map/while/body/eval_jaxpr/ppermute | solution.py:25
  305.0 8.5 %collective-permute-start = (f32[1,2048]{1,0:T(1,128)S(1)}, f32[1,2048]{1,0:T(1,128)S(1)}, u32[]{:S(2)}, u32[]{:S(2)}) collective-permute-start(f32[1,2048]{1,0:T(1,128)S(1)} %get-tuple-element.283), channel_id=1, source_target_pairs={{1,0},{2,1},{3,2},{4,3},{5,4},{6,5},{7,6},{8,7},{9,8},{10,9},{11,1... | collective-permute-start | bytes 24584 | tf_op jit(solution)/shard_map/while/body/eval_jaxpr/ppermute | solution.py:17
  325.0 8.9 %collective-permute-start.4 = (f32[32,2048]{1,0:T(8,128)S(1)}, f32[32,2048]{1,0:T(8,128)S(1)}, u32[]{:S(2)}, u32[]{:S(2)}) collective-permute-start(f32[32,2048]{1,0:T(8,128)S(1)} %fusion.408), channel_id=1, source_target_pairs={{0,16},{16,32},{32,48},{48,64},{64,80},{80,96},{96,112},{112,128},... | collective-permute-start | bytes 786440 | tf_op jit(solution)/shard_map/while/body/eval_jaxpr/ppermute | solution.py:25
  334.0 8.5 %collective-permute-start = (f32[1,2048]{1,0:T(1,128)S(1)}, f32[1,2048]{1,0:T(1,128)S(1)}, u32[]{:S(2)}, u32[]{:S(2)}) collective-permute-start(f32[1,2048]{1,0:T(1,128)S(1)} %get-tuple-element.283), channel_id=1, source_target_pairs={{1,0},{2,1},{3,2},{4,3},{5,4},{6,5},{7,6},{8,7},{9,8},{10,9},{11,1... | collective-permute-start | bytes 24584 | tf_op jit(solution)/shard_map/while/body/eval_jaxpr/ppermute | solution.py:17
  354.0 8.9 %collective-permute-start.4 = (f32[32,2048]{1,0:T(8,128)S(1)}, f32[32,2048]{1,0:T(8,128)S(1)}, u32[]{:S(2)}, u32[]{:S(2)}) collective-permute-start(f32[32,2048]{1,0:T(8,128)S(1)} %fusion.408), channel_id=1, source_target_pairs={{0,16},{16,32},{32,48},{48,64},{64,80},{80,96},{96,112},{112,128},... | collective-permute-start | bytes 786440 | tf_op jit(solution)/shard_map/while/body/eval_jaxpr/ppermute | solution.py:25
  363.0 8.5 %collective-permute-start = (f32[1,2048]{1,0:T(1,128)S(1)}, f32[1,2048]{1,0:T(1,128)S(1)}, u32[]{:S(2)}, u32[]{:S(2)}) collective-permute-start(f32[1,2048]{1,0:T(1,128)S(1)} %get-tuple-element.283), channel_id=1, source_target_pairs={{1,0},{2,1},{3,2},{4,3},{5,4},{6,5},{7,6},{8,7},{9,8},{10,9},{11,1... | collective-permute-start | bytes 24584 | tf_op jit(solution)/shard_map/while/body/eval_jaxpr/ppermute | solution.py:17
  383.0 8.9 %collective-permute-start.4 = (f32[32,2048]{1,0:T(8,128)S(1)}, f32[32,2048]{1,0:T(8,128)S(1)}, u32[]{:S(2)}, u32[]{:S(2)}) collective-permute-start(f32[32,2048]{1,0:T(8,128)S(1)} %fusion.408), channel_id=1, source_target_pairs={{0,16},{16,32},{32,48},{48,64},{64,80},{80,96},{96,112},{112,128},... | collective-permute-start | bytes 786440 | tf_op jit(solution)/shard_map/while/body/eval_jaxpr/ppermute | solution.py:25
  392.0 8.5 %collective-permute-start = (f32[1,2048]{1,0:T(1,128)S(1)}, f32[1,2048]{1,0:T(1,128)S(1)}, u32[]{:S(2)}, u32[]{:S(2)}) collective-permute-start(f32[1,2048]{1,0:T(1,128)S(1)} %get-tuple-element.283), channel_id=1, source_target_pairs={{1,0},{2,1},{3,2},{4,3},{5,4},{6,5},{7,6},{8,7},{9,8},{10,9},{11,1... | collective-permute-start | bytes 24584 | tf_op jit(solution)/shard_map/while/body/eval_jaxpr/ppermute | solution.py:17
  412.0 8.9 %collective-permute-start.4 = (f32[32,2048]{1,0:T(8,128)S(1)}, f32[32,2048]{1,0:T(8,128)S(1)}, u32[]{:S(2)}, u32[]{:S(2)}) collective-permute-start(f32[32,2048]{1,0:T(8,128)S(1)} %fusion.408), channel_id=1, source_target_pairs={{0,16},{16,32},{32,48},{48,64},{64,80},{80,96},{96,112},{112,128},... | collective-permute-start | bytes 786440 | tf_op jit(solution)/shard_map/while/body/eval_jaxpr/ppermute | solution.py:25
  441.1 8.9 %collective-permute-start.4 = (f32[32,2048]{1,0:T(8,128)S(1)}, f32[32,2048]{1,0:T(8,128)S(1)}, u32[]{:S(2)}, u32[]{:S(2)}) collective-permute-start(f32[32,2048]{1,0:T(8,128)S(1)} %fusion.408), channel_id=1, source_target_pairs={{0,16},{16,32},{32,48},{48,64},{64,80},{80,96},{96,112},{112,128},... | collective-permute-start | bytes 786440 | tf_op jit(solution)/shard_map/while/body/eval_jaxpr/ppermute | solution.py:25
  470.1 8.9 %collective-permute-start.4 = (f32[32,2048]{1,0:T(8,128)S(1)}, f32[32,2048]{1,0:T(8,128)S(1)}, u32[]{:S(2)}, u32[]{:S(2)}) collective-permute-start(f32[32,2048]{1,0:T(8,128)S(1)} %fusion.408), channel_id=1, source_target_pairs={{0,16},{16,32},{32,48},{48,64},{64,80},{80,96},{96,112},{112,128},... | collective-permute-start | bytes 786440 | tf_op jit(solution)/shard_map/while/body/eval_jaxpr/ppermute | solution.py:25
  479.0 8.5 %collective-permute-start = (f32[1,2048]{1,0:T(1,128)S(1)}, f32[1,2048]{1,0:T(1,128)S(1)}, u32[]{:S(2)}, u32[]{:S(2)}) collective-permute-start(f32[1,2048]{1,0:T(1,128)S(1)} %get-tuple-element.283), channel_id=1, source_target_pairs={{1,0},{2,1},{3,2},{4,3},{5,4},{6,5},{7,6},{8,7},{9,8},{10,9},{11,1... | collective-permute-start | bytes 24584 | tf_op jit(solution)/shard_map/while/body/eval_jaxpr/ppermute | solution.py:17
  499.1 8.9 %collective-permute-start.4 = (f32[32,2048]{1,0:T(8,128)S(1)}, f32[32,2048]{1,0:T(8,128)S(1)}, u32[]{:S(2)}, u32[]{:S(2)}) collective-permute-start(f32[32,2048]{1,0:T(8,128)S(1)} %fusion.408), channel_id=1, source_target_pairs={{0,16},{16,32},{32,48},{48,64},{64,80},{80,96},{96,112},{112,128},... | collective-permute-start | bytes 786440 | tf_op jit(solution)/shard_map/while/body/eval_jaxpr/ppermute | solution.py:25
  508.1 8.5 %collective-permute-start = (f32[1,2048]{1,0:T(1,128)S(1)}, f32[1,2048]{1,0:T(1,128)S(1)}, u32[]{:S(2)}, u32[]{:S(2)}) collective-permute-start(f32[1,2048]{1,0:T(1,128)S(1)} %get-tuple-element.283), channel_id=1, source_target_pairs={{1,0},{2,1},{3,2},{4,3},{5,4},{6,5},{7,6},{8,7},{9,8},{10,9},{11,1... | collective-permute-start | bytes 24584 | tf_op jit(solution)/shard_map/while/body/eval_jaxpr/ppermute | solution.py:17
  528.1 8.9 %collective-permute-start.4 = (f32[32,2048]{1,0:T(8,128)S(1)}, f32[32,2048]{1,0:T(8,128)S(1)}, u32[]{:S(2)}, u32[]{:S(2)}) collective-permute-start(f32[32,2048]{1,0:T(8,128)S(1)} %fusion.408), channel_id=1, source_target_pairs={{0,16},{16,32},{32,48},{48,64},{64,80},{80,96},{96,112},{112,128},... | collective-permute-start | bytes 786440 | tf_op jit(solution)/shard_map/while/body/eval_jaxpr/ppermute | solution.py:25
  557.1 8.9 %collective-permute-start.4 = (f32[32,2048]{1,0:T(8,128)S(1)}, f32[32,2048]{1,0:T(8,128)S(1)}, u32[]{:S(2)}, u32[]{:S(2)}) collective-permute-start(f32[32,2048]{1,0:T(8,128)S(1)} %fusion.408), channel_id=1, source_target_pairs={{0,16},{16,32},{32,48},{48,64},{64,80},{80,96},{96,112},{112,128},... | collective-permute-start | bytes 786440 | tf_op jit(solution)/shard_map/while/body/eval_jaxpr/ppermute | solution.py:25
  586.1 8.9 %collective-permute-start.4 = (f32[32,2048]{1,0:T(8,128)S(1)}, f32[32,2048]{1,0:T(8,128)S(1)}, u32[]{:S(2)}, u32[]{:S(2)}) collective-permute-start(f32[32,2048]{1,0:T(8,128)S(1)} %fusion.408), channel_id=1, source_target_pairs={{0,16},{16,32},{32,48},{48,64},{64,80},{80,96},{96,112},{112,128},... | collective-permute-start | bytes 786440 | tf_op jit(solution)/shard_map/while/body/eval_jaxpr/ppermute | solution.py:25
  615.2 8.9 %collective-permute-start.4 = (f32[32,2048]{1,0:T(8,128)S(1)}, f32[32,2048]{1,0:T(8,128)S(1)}, u32[]{:S(2)}, u32[]{:S(2)}) collective-permute-start(f32[32,2048]{1,0:T(8,128)S(1)} %fusion.408), channel_id=1, source_target_pairs={{0,16},{16,32},{32,48},{48,64},{64,80},{80,96},{96,112},{112,128},... | collective-permute-start | bytes 786440 | tf_op jit(solution)/shard_map/while/body/eval_jaxpr/ppermute | solution.py:25
  (94 other events, 689.4 us)
where the time goes:
time: 653 us; the launch traced here: 649 us
  starting transfers between devices  387 us (59%)
  waiting for transfers between devices  225 us (34%)
  other arithmetic  23 us (4%)
  local copies, waits for them, and re-layouts  12.4 us (2%)
    ppermute x48, starting transfers between devices, with_halo(): before = lax.ppermute(last, axis, up)  211 us
    ppermute x48, starting transfers between devices, with_halo(): after = lax.ppermute(initial, axis, down)  143 us
    ppermute x17, waiting for transfers between devices, shifted(): return lax.ppermute(block, axis, route)  118 us
    ppermute x48, waiting for transfers between devices, with_halo(): after = lax.ppermute(initial, axis, down)  70.9 us
    ppermute x48, waiting for transfers between devices, with_halo(): before = lax.ppermute(last, axis, up)  36 us
    ppermute x17, starting transfers between devices, shifted(): return lax.ppermute(block, axis, route)  32.6 us
  transfers between devices with their start and end apart: 113, of which 65 were waited for; matrix products, arithmetic and copies ran while one was open for 1% of the time, Pallas kernels for 0%

commit v1 on v0

v1 whole, which is shorter than its diff:
```python
import functools

import jax
import jax.numpy as jnp
from jax import lax
from jax.experimental import pallas as pl
from jax.experimental.pallas import tpu as pltpu
from jax.sharding import PartitionSpec as P

MESH = pl.DeviceIdType.MESH
F32 = jnp.float32

OFF = 16
ROWS = 64
MAIN = 32
HALO = 12
TILE = 128

Z0, Z1, R1 = 4, 5, 6
C0 = 7
NW = 9

NSEM = 64


def kernel(
    cg, init, dif, vel, rea, src,
    out,
    st, co, cc, w, fc, v, obuf,
    lsem, ssem, rsem, csend, crecv, xsend, xrecv,
):
    t = lax.axis_index("tm")
    s = lax.axis_index("space")
    z, core = t // 2, t % 2
    odd = s % 2 == 1
    has_up, has_dn = s > 0, s < 15

    lane = lax.broadcasted_iota(jnp.int32, (8, 128), 1)
    first_lane, last_lane = lane == 0, lane == 127

    loads = [
        (None, dif, st.at[0, pl.ds(2 * TILE, 512)]),
        (None, vel, st.at[pl.ds(1, 2), pl.ds(2 * TILE, 512)]),
        (None, rea, st.at[3, pl.ds(2 * TILE, 512)]),
        (None, src, st.at[4, pl.ds(2 * TILE, 512)]),
        (None, cg.at[0], st.at[6, pl.ds(2 * TILE, 512)]),
        (t == 0, init, st.at[5, pl.ds(2 * TILE, 512)]),
    ]

    def when(cond, body):
        if cond is None:
            body()
        else:
            pl.when(cond)(body)

    for i, (cond, a, b) in enumerate(loads):
        when(cond, lambda a=a, b=b, i=i: pltpu.make_async_copy(a, b, lsem.at[i]).start())

    partners = []
    for dt in (-2, -1, 0, 1, 2):
        for ds in (-1, 0, 1):
            if dt == 0 and ds == 0:
                continue
            ok = (t + dt >= 0) & (t + dt <= 15) & (s + ds >= 0) & (s + ds <= 15)
            partners.append((ok, t + dt, s + ds))
    barrier = pltpu.get_barrier_semaphore()
    count = 0
    for ok, pt, ps in partners:
        @pl.when(ok)
        def _(pt=pt, ps=ps):
            pl.semaphore_signal(barrier, inc=1, device_id=(pt, ps), device_id_type=MESH)
        count = count + ok.astype(jnp.int32)

    zero = jnp.zeros((8, 128), F32)

    def clear(at_stage, rows):
        def body(i, _):
            for q in range(7):
                st[q, pl.ds(at_stage + i * 8, 8), :] = zero
            return 0

        lax.fori_loop(0, 32, body, 0)

        def rows_body(i, _):
            for b in (Z0, Z1):
                for h in range(2):
                    w[b, OFF + rows + i, h] = zero
            for h in range(2):
                v[0, OFF + rows + i, h] = zero
            return 0

        lax.fori_loop(0, HALO, rows_body, 0)

    pl.when(s == 0)(lambda: clear(0, -HALO))
    pl.when(s == 15)(lambda: clear(6 * TILE, MAIN))

    pl.semaphore_wait(barrier, count)

    used = [0]

    def remote(source, dest, device, sends, receives):
        i = used[0]
        used[0] += 1
        cp = pltpu.make_async_remote_copy(
            src_ref=source, dst_ref=dest, send_sem=ssem.at[i], recv_sem=rsem.at[i],
            device_id=device, device_id_type=MESH,
        )
        return sends, receives, cp

    def start(copies):
        for sends, _, cp in copies:
            pl.when(sends)(lambda cp=cp: cp.start())

    def wait_recv(copies):
        for _, receives, cp in copies:
            pl.when(receives)(lambda cp=cp: cp.wait_recv())

    def wait_send(copies):
        for sends, _, cp in copies:
            pl.when(sends)(lambda cp=cp: cp.wait_send())

    later_t, had_t = t < 15, t > 0
    yes = t >= 0
    near, far = [], []
    for group, up_from, up_to, dn_from, dn_to in (
        (near, 3 * TILE, 1 * TILE, 0, 6 * TILE),
        (far, 2 * TILE, 0, TILE, 7 * TILE),
    ):
        for a, b in ((dif, 0), (vel, None), (rea, 3), (src, 4)):
            def part(at, a=a):
                return a.at[:, pl.ds(at, TILE)] if len(a.shape) == 3 else a.at[pl.ds(at, TILE)]

            def stage(at, b=b):
                return st.at[pl.ds(1, 2), pl.ds(at, TILE)] if b is None else st.at[b, pl.ds(at, TILE)]

            group.append(remote(part(up_from), stage(up_to), (t, s + 1), has_dn, has_up))
            group.append(remote(part(dn_from), stage(dn_to), (t, s - 1), has_up, has_dn))
    own = [
        remote(cg.at[0, pl.ds(3 * TILE, TILE)], st.at[6, pl.ds(TILE, TILE)], (t, s + 1), has_dn, has_up),
        remote(cg.at[0, pl.ds(0, TILE)], st.at[6, pl.ds(6 * TILE, TILE)], (t, s - 1), has_up, has_dn),
    ]
    nxt = [
        remote(cg.at[1], st.at[5, pl.ds(2 * TILE, 512)], (t + 1, s), later_t, had_t),
        remote(cg.at[1, pl.ds(3 * TILE, TILE)], st.at[5, pl.ds(TILE, TILE)], (t + 1, s + 1), later_t & has_dn, had_t & has_up),
        remote(cg.at[1, pl.ds(0, TILE)], st.at[5, pl.ds(6 * TILE, TILE)], (t + 1, s - 1), later_t & has_up, had_t & has_dn),
    ]
    ini = [
        remote(init.at[pl.ds(3 * TILE, TILE)], st.at[5, pl.ds(TILE, TILE)], (t, s + 1), (t == 0) & has_dn, (t == 0) & has_up),
        remote(init.at[pl.ds(0, TILE)], st.at[5, pl.ds(6 * TILE, TILE)], (t, s - 1), (t == 0) & has_up, (t == 0) & has_dn),
    ]
    first = near + own + ini + nxt
    start(first)
    start(far)

    def staged(q, tile, r8, h):
        return st[q, pl.ds(tile * TILE + r8 + 8 * h, 8, stride=16), :]

    def coefficients(tile_lo, tiles):
        def body(i, _):
            tile = tile_lo + i
            for r8 in range(8):
                row = tile * 8 + r8
                for h in range(2):
                    d, b, c, k, sr = [staged(q, tile, r8, h) for q in range(5)]
                    u = d + jnp.maximum(b, 0.0)
                    n = d - jnp.minimum(b, 0.0)
                    le = d + jnp.maximum(c, 0.0)
                    ri = d - jnp.minimum(c, 0.0)
                    a = k - ((u + n) + (le + ri))
                    co[0, row, h] = 1.0 + a
                    co[1, row, h] = k
                    co[2, row, h] = u
                    co[3, row, h] = n
                    co[4, row, h] = le
                    co[5, row, h] = ri
                    co[6, row, h] = sr
            return 0

        lax.fori_loop(0, tiles, body, 0)

    def coarse_coefficients():
        def body(i, _):
            for j in range(4):
                row = OFF - 4 + i * 4 + j
                for h in range(2):
                    k, u, n, le, ri, sr = [8.0 * co[q, row, h] for q in range(1, 7)]
                    cc[0, row, h] = 1.0 + (k - ((u + n) + (le + ri)))
                    for q, x in enumerate((k, u, n, le, ri, sr)):
                        cc[1 + q, row, h] = x
            return 0

        lax.fori_loop(0, 10, body, 0)

    def field(q, dest, tile_lo, tiles):
        def body(i, _):
            tile = tile_lo + i
            for r8 in range(8):
                for h in range(2):
                    w[dest, tile * 8 + r8, h] = staged(q, tile, r8, h)
            return 0

        lax.fori_loop(0, tiles, body, 0)

    def sides(a, b):
        ra, rb = pltpu.roll(a, 1, 1), pltpu.roll(b, 1, 1)
        la = jnp.where(first_lane, pltpu.roll(rb, 1, 0), ra)
        lb = jnp.where(first_lane, ra, rb)
        qa, qb = pltpu.roll(a, 127, 1), pltpu.roll(b, 127, 1)
        ga = jnp.where(last_lane, qb, qa)
        gb = jnp.where(last_lane, pltpu.roll(qa, 7, 0), qb)
        return (la, lb), (ga, gb)

    def step(state, coef, base, n, emit):
        load = lambda row: [state[row, h] for h in range(2)]
        up, ce = load(base - 1), load(base)
        for r in range(n):
            row = base + r
            dn = load(row + 1)
            left, right = sides(*ce)
            for h in range(2):
                a, k, u, d, le, ri, sr = [coef[q, row, h] for q in range(7)]
                x = ce[h]
                y = x * (a - k * (x * x)) + sr
                y = y + u * up[h] + d * dn[h]
                y = y + le * left[h] + ri * right[h]
                emit(r, row, h, y, x)
            up, ce = ce, dn

    for i, (cond, a, b) in enumerate(loads):
        when(cond, lambda a=a, b=b, i=i: pltpu.make_async_copy(a, b, lsem.at[i]).wait())
    coefficients(2, 4)
    field(6, 2, 2, 4)
    wait_recv(near + own + ini + nxt)
    coefficients(1, 1)
    coefficients(6, 1)
    field(6, 2, 1, 1)
    field(6, 2, 6, 1)
    field(5, 0, 1, 6)

    edge_r0 = [
        remote(w.at[Z1, pl.ds(OFF + MAIN - HALO, HALO)], w.at[Z1, pl.ds(OFF - HALO, HALO)], (t, s + 1), has_dn, has_up),
        remote(w.at[Z1, pl.ds(OFF, HALO)], w.at[Z1, pl.ds(OFF + MAIN, HALO)], (t, s - 1), has_up, has_dn),
    ]
    move_r1 = [
        remote(w.at[R1, pl.ds(OFF, MAIN)], w.at[Z0, pl.ds(OFF, MAIN)], (t + 1, s), later_t, had_t),
        remote(w.at[R1, pl.ds(OFF + MAIN - HALO, HALO)], w.at[Z0, pl.ds(OFF - HALO, HALO)], (t + 1, s + 1), later_t & has_dn, had_t & has_up),
        remote(w.at[R1, pl.ds(OFF, HALO)], w.at[Z0, pl.ds(OFF + MAIN, HALO)], (t + 1, s - 1), later_t & has_up, had_t & has_dn),
    ]

    def relax(i, _):
        f = 1 - i

        def one(k, _):
            a = 2 * f + k % 2
            b = 2 * f + 1 - k % 2

            def emit(r, row, h, y, x):
                w[b, row, h] = y

            step(w.at[a], co, OFF - 7, 46, emit)
            return 0

        lax.fori_loop(0, 7, one, 0)
        dest = Z1 + f

        def emit(r, row, h, y, x):
            w[dest, row, h] = y

        step(w.at[2 * f + 1], co, OFF, MAIN, emit)
        pl.when(f == 1)(lambda: start(move_r1))
        return 0

    lax.fori_loop(0, 2, relax, 0)
    start(edge_r0)
    wait_recv(far)
    coefficients(0, 1)
    coefficients(7, 1)
    coarse_coefficients()

    def again(i, _):
        f = 1 - i
        pl.when(f == 1)(lambda: wait_recv(edge_r0))
        pl.when(f == 0)(lambda: wait_recv(move_r1))

        def emit_first(r, row, h, y, x):
            w[2 * f, row, h] = y
            if 7 <= r < 47:
                w[C0 + f, row, h] = 8.0 * y - 7.0 * x

        step(w.at[Z0 + f], co, OFF - 11, 54, emit_first)

        def one(k, _):
            a = 2 * f + k % 2
            b = 2 * f + 1 - k % 2

            def emit(r, row, h, y, x):
                w[b, row, h] = y

            step(w.at[a], co, OFF - 10, 52, emit)
            return 0

        lax.fori_loop(0, 6, one, 0)

        def emit_last(r, row, h, y, x):
            w[2 * f + 1, row, h] = y
            fc[2 * core + f, row, h] = y - w[C0 + f, row, h]

        step(w.at[2 * f], co, OFF - 4, 40, emit_last)
        return 0

    lax.fori_loop(0, jnp.where(t == 0, 1, 2), again, 0)

    give_f = [
        remote(fc.at[pl.ds(2, 2), pl.ds(OFF - 4, 40)], fc.at[pl.ds(2, 2), pl.ds(OFF - 4, 40)], (t - 1, s), core == 1, core == 0),
    ]
    start(give_f)

    def chunk_row(m):
        return OFF + jnp.where(odd, 4 * m, 28 - 4 * m)

    def main_copy(m):
        rows = pl.ds(chunk_row(m), 4)
        return pltpu.make_async_remote_copy(
            src_ref=v.at[4, rows], dst_ref=v.at[0, rows], send_sem=csend.at[m], recv_sem=crecv.at[m],
            device_id=(t + 2, s), device_id_type=MESH,
        )

    def edge_copy(i, from_row, to_row, ds):
        return pltpu.make_async_remote_copy(
            src_ref=v.at[4, pl.ds(from_row, 4)], dst_ref=v.at[0, pl.ds(to_row, 4)],
            send_sem=csend.at[8 + i], recv_sem=crecv.at[8 + i],
            device_id=(t + 2, s + ds), device_id_type=MESH,
        )

    low_from, low_to = OFF, OFF + MAIN
    top_from, top_to = OFF + MAIN - 4, OFF - 4

    def give_copy(m):
        rows = pl.ds(chunk_row(m), 4)
        return pltpu.make_async_remote_copy(
            src_ref=v.at[pl.ds(3, 2), rows], dst_ref=v.at[pl.ds(3, 2), rows],
            send_sem=xsend.at[m], recv_sem=xrecv.at[m], device_id=(t + 1, s), device_id_type=MESH,
        )

    def to_out(state, o, row):
        tile = (row - OFF) // 8
        r8 = (row - OFF) % 8
        for h in range(2):
            obuf[o, pl.ds(tile * TILE + r8 + 8 * h, 8, stride=16), :] = state[row, h]

    def send_edges(m):
        pl.when((m == 0) & odd)(lambda: edge_copy(0, low_from, low_to, -1).start())
        pl.when((m == 0) & jnp.logical_not(odd))(lambda: edge_copy(0, top_from, top_to, 1).start())
        pl.when((m == 7) & odd & has_dn)(lambda: edge_copy(1, top_from, top_to, 1).start())
        pl.when((m == 7) & jnp.logical_not(odd) & has_up)(lambda: edge_copy(1, low_from, low_to, -1).start())

    end_edge = jnp.where(odd, has_dn, has_up)

    def chain():
        wait_recv(give_f)
        pl.when(z == 0)(lambda: copy_rows(3, v, 2, OFF - 4, 40))

        def level(k, base, n):
            def emit(r, row, h, y, x):
                v[k, row, h] = y + fc[k - 1, row, h]

            step(v.at[k - 1], cc, base, n, emit)

        def base_of(i, k):
            return OFF + jnp.where(odd, 4 * i - 4 - k, 32 - 4 * i + k)

        def turn(i, _):
            @pl.when(z > 0)
            def _():
                @pl.when(i == 1)
                def _():
                    edge_copy(0, low_from, low_to, 0).wait_recv()

                pl.when(i < 9)(lambda: main_copy(jnp.minimum(i - 1, 7)).wait_recv())
                pl.when((i == 9) & end_edge)(lambda: edge_copy(1, low_from, low_to, 0).wait_recv())
                pl.when(i == 1)(lambda: level(1, base_of(0, 1), 4))
                level(1, base_of(i, 1), 4)
                level(2, base_of(i, 2), 4)

            level(3, base_of(i, 3), 4)

            @pl.when(i > 1)
            def _():
                level(4, base_of(i, 4), 4)
                m = i - 2

                @pl.when(z < 7)
                def _():
                    main_copy(m).start()
                    send_edges(m)

                give_copy(m).start()

            return 0

        lax.fori_loop(1, 10, turn, 0)

    def copy_rows(source, to, dest, base, n):
        def body(i, _):
            for j in range(4):
                for h in range(2):
                    to[dest, base + 4 * i + j, h] = w[source, base + 4 * i + j, h]
            return 0

        lax.fori_loop(0, n // 4, body, 0)

    def finish_first():
        pl.when(z == 0)(lambda: copy_rows(Z1, v, 1, OFF, MAIN))

        def body(i, _):
            for j in range(4):
                to_out(v.at[1], 0, OFF + 4 * i + j)
                to_out(v.at[2], 1, OFF + 4 * i + j)
            return 0

        lax.fori_loop(0, 8, body, 0)

    def finish_second():
        def body(m, _):
            give_copy(m).wait_recv()
            for j in range(4):
                to_out(v.at[3], 0, chunk_row(m) + j)
                to_out(v.at[4], 1, chunk_row(m) + j)
            return 0

        lax.fori_loop(0, 8, body, 0)

    @pl.when(core == 0)
    def _():
        chain()
        finish_first()

    pl.when(core == 1)(finish_second)
    done = pltpu.make_async_copy(obuf, out, lsem.at[0])
    done.start()

    wait_send(near + far + own + ini + nxt + edge_r0 + move_r1 + give_f)

    @pl.when(core == 0)
    def _():
        def drain(m, _):
            pl.when(z < 7)(lambda: main_copy(m).wait_send())
            give_copy(m).wait_send()
            return 0

        lax.fori_loop(0, 8, drain, 0)
        pl.when(z < 7)(lambda: edge_copy(0, low_from, low_to, 0).wait_send())
        pl.when((z < 7) & end_edge)(lambda: edge_copy(1, low_from, low_to, 0).wait_send())

    done.wait()


def tiles(x):
    lead = x.shape[:-2]
    n = len(lead)
    y = x.reshape(lead + (4, 8, 16, 128))
    y = y.transpose(tuple(range(n)) + (n, n + 2, n + 1, n + 3))
    return y.reshape(lead + (512, 128))


def shards(coarse_guess, initial, diffusion, velocity, reaction, source):
    hbm = pl.BlockSpec(memory_space=pl.ANY)
    state = (2, 8, 128)
    out = pl.pallas_call(
        kernel,
        out_shape=jax.ShapeDtypeStruct((2, 512, 128), F32),
        in_specs=[hbm] * 6,
        out_specs=hbm,
        scratch_shapes=[
            pltpu.VMEM((7, 8 * TILE, 128), F32),
            pltpu.VMEM((7, ROWS) + state, F32),
            pltpu.VMEM((7, ROWS) + state, F32),
            pltpu.VMEM((NW, ROWS) + state, F32),
            pltpu.VMEM((4, ROWS) + state, F32),
            pltpu.VMEM((5, ROWS) + state, F32),
            pltpu.VMEM((2, 512, 128), F32),
            pltpu.SemaphoreType.DMA((8,)),
            pltpu.SemaphoreType.DMA((NSEM,)),
            pltpu.SemaphoreType.DMA((NSEM,)),
            pltpu.SemaphoreType.DMA((10,)),
            pltpu.SemaphoreType.DMA((10,)),
            pltpu.SemaphoreType.DMA((8,)),
            pltpu.SemaphoreType.DMA((8,)),
        ],
        compiler_params=pltpu.CompilerParams(
            collective_id=0, has_side_effects=True, vmem_limit_bytes=48 * 2**20
        ),
    )(tiles(coarse_guess), tiles(initial), tiles(diffusion), tiles(velocity), tiles(reaction), tiles(source))
    out = out.reshape(2, 4, 16, 8, 128).transpose(0, 1, 3, 2, 4)
    return out.reshape(2, 32, 2048)


def solution(mesh):
    return jax.shard_map(
        shards,
        mesh=mesh,
        in_specs=(
            P("tm", "space", None),
            P("space", None),
            P("space", None),
            P(None, "space", None),
            P("space", None),
            P("space", None),
        ),
        out_specs=P("tm", "space", None),
        check_vma=False,
    )
```

time: 653 us -> 126 us (0.19)
  the two profiles are of different devices: /device:TPU:142 before, /device:TPU:249 now
where the time goes in v1:
time: 126 us
  Pallas kernels  119 us (94%)
  local copies, waits for them, and re-layouts  6.68 us (5%)
    pallas_call x1, Pallas kernels, shards(): pl.pallas_call(kernel, out_shape=jax.ShapeDtypeStruct((2, 512, 128), F32)...  119 us
    unnamed x13, local copies, waits for them, and re-layouts  6.68 us

profile of v1, /device:TPU:249, one launch (start us, length us, event | category | flops | bytes accessed | tf_op | source)
XLA Modules:
  0.0 125.7 jit_solution(5657223583853454060)
XLA Ops:
  0.0 0.0 copy-start
  0.0 1.0 copy-done
  1.0 0.0 copy-start.1
  1.0 1.0 copy-done.1
  2.1 0.0 copy-start.2
  2.1 0.9 copy-done.2
  3.0 0.0 copy-start.3
  3.0 0.9 copy-done.3
  4.0 0.0 copy-start.4
  4.0 0.9 copy-done.4
  4.9 0.0 copy-start.5
  4.9 0.9 copy-done.5
  5.9 119.0 %shard_map.64 = f32[2,512,128]{2,1,0:T(8,128)S(1)} custom-call(f32[2,512,128]{2,1,0:T(8,128)S(1)} %bitcast.36, f32[512,128]{1,0:T(8,128)S(1)} %bitcast.38, f32[512,128]{1,0:T(8,128)S(1)} %bitcast.39, f32[2,512,128]{2,1,0:T(8,128)S(1)} %bitcast.37, f32[512,128]{1,0:T(8,128)S(1)} %bitcast.40, f32[512,128]{1,0:T(8,128)S(1)} %bitcast.41), custom_call_target="tpu_custom_call" | custom-call | tf_op jit(solution)/shard_map/pallas_call | solution.py:469
  124.9 0.8 copy.8
Async XLA Ops:
  0.0 1.0 copy-start
  1.0 1.0 copy-start.1
  2.1 0.9 copy-start.2
  3.0 0.9 copy-start.3
  4.0 0.9 copy-start.4
  4.9 0.9 copy-start.5

commit v2 on v1

v2 whole, which is shorter than its diff:
```python
import functools

import jax
import jax.numpy as jnp
from jax import lax
from jax.experimental import pallas as pl
from jax.experimental.pallas import tpu as pltpu
from jax.sharding import PartitionSpec as P

MESH = pl.DeviceIdType.MESH
F32 = jnp.float32

OFF = 16
ROWS = 64
MAIN = 32
HALO = 12
TILE = 128


NSEM = 64


def kernel(
    cg, init, dif, vel, rea, src,
    out,
    st, co, cc, ping, pong, again_in, first_coarse, fc, v, prev, obuf,
    lsem, ssem, rsem, esend, erecv, csend, crecv, xsend, xrecv, fsend, frecv,
):
    t = lax.axis_index("tm")
    s = lax.axis_index("space")
    t_last, s_last = lax.axis_size("tm") - 1, lax.axis_size("space") - 1
    z_last = t_last // 2
    z, core = t // 2, t % 2
    odd = s % 2 == 1
    has_up, has_dn = s > 0, s < s_last
    origin = t == t_last

    lane = lax.broadcasted_iota(jnp.int32, (8, 128), 1)
    first_lane, last_lane = lane == 0, lane == 127

    loads = [
        (None, dif, st.at[0, pl.ds(2 * TILE, 512)]),
        (None, vel, st.at[pl.ds(1, 2), pl.ds(2 * TILE, 512)]),
        (None, rea, st.at[3, pl.ds(2 * TILE, 512)]),
        (None, src, st.at[4, pl.ds(2 * TILE, 512)]),
        (t < t_last, cg.at[0], st.at[5, pl.ds(2 * TILE, 512)]),
        (t < t_last, cg.at[1], st.at[6, pl.ds(2 * TILE, 512)]),
        (origin, init, st.at[5, pl.ds(2 * TILE, 512)]),
    ]

    def when(cond, body):
        if cond is None:
            body()
        else:
            pl.when(cond)(body)

    for i, (cond, a, b) in enumerate(loads):
        when(cond, lambda a=a, b=b, i=i: pltpu.make_async_copy(a, b, lsem.at[i]).start())

    partners = []

    def partner(ok, pt, ps):
        partners.append((ok & (ps >= 0) & (ps <= s_last), pt, ps))

    for ds in (-1, 1):
        partner(t >= 0, t, s + ds)
    for ds in (-1, 0, 1):
        partner((core == 0) & (z > 0), t - 2, s + ds)
        partner((core == 0) & (z < z_last), t + 2, s + ds)
    partner(t > 0, t - 1, s)
    partner(t < t_last, t + 1, s)
    partner((t == 0) | origin, t_last - t, s)
    barrier = pltpu.get_barrier_semaphore()
    count = 0
    for ok, pt, ps in partners:
        @pl.when(ok)
        def _(pt=pt, ps=ps):
            pl.semaphore_signal(barrier, inc=1, device_id=(pt, ps), device_id_type=MESH)
        count = count + ok.astype(jnp.int32)

    zero = jnp.zeros((8, 128), F32)

    def clear(at_stage, rows):
        def body(i, _):
            for q in range(7):
                st[q, pl.ds(at_stage + i * 8, 8), :] = zero
            return 0

        lax.fori_loop(0, 32, body, 0)

        def rows_body(i, _):
            for b in range(2):
                for h in range(2):
                    again_in[b, OFF + rows + i, h] = zero
            for h in range(2):
                v[0, OFF + rows + i, h] = zero
            return 0

        lax.fori_loop(0, HALO, rows_body, 0)

    pl.when(s == 0)(lambda: clear(0, -HALO))
    pl.when(s == s_last)(lambda: clear(6 * TILE, MAIN))

    pl.semaphore_wait(barrier, count)

    used = [0]

    def remote(source, dest, device, sends, receives):
        i = used[0]
        used[0] += 1
        cp = pltpu.make_async_remote_copy(
            src_ref=source, dst_ref=dest, send_sem=ssem.at[i], recv_sem=rsem.at[i],
            device_id=device, device_id_type=MESH,
        )
        return sends, receives, cp

    def start(copies):
        for sends, _, cp in copies:
            pl.when(sends)(lambda cp=cp: cp.start())

    def wait_recv(copies):
        for _, receives, cp in copies:
            pl.when(receives)(lambda cp=cp: cp.wait_recv())

    def wait_send(copies):
        for sends, _, cp in copies:
            pl.when(sends)(lambda cp=cp: cp.wait_send())

    near, far, near_on, far_on = [], [], [], []
    half = pl.multiple_of(core * (TILE // 2), TILE // 2)
    sibling = (t + 1 - 2 * core, s)
    for group, onward, up_from, up_to, dn_from, dn_to in (
        (near, near_on, 3 * TILE, 1 * TILE, 0, 6 * TILE),
        (far, far_on, 2 * TILE, 0, TILE, 7 * TILE),
    ):
        for a, b in ((dif, 0), (vel, None), (rea, 3), (src, 4)):
            def part(at, a=a):
                rows = pl.ds(at + half, TILE // 2)
                return a.at[:, rows] if len(a.shape) == 3 else a.at[rows]

            def stage(at, b=b):
                rows = pl.ds(at + half, TILE // 2)
                return st.at[pl.ds(1, 2), rows] if b is None else st.at[b, rows]

            group.append(remote(part(up_from), stage(up_to), (t, s + 1), has_dn, has_up))
            group.append(remote(part(dn_from), stage(dn_to), (t, s - 1), has_up, has_dn))
            onward.append(remote(stage(up_to), stage(up_to), sibling, has_up, has_up))
            onward.append(remote(stage(dn_to), stage(dn_to), sibling, has_dn, has_dn))
    fields = []
    for a, b, mine in ((cg.at[0], 5, t < t_last), (cg.at[1], 6, t < t_last), (init, 5, origin)):
        fields += [
            remote(a.at[pl.ds(3 * TILE, TILE)], st.at[b, pl.ds(TILE, TILE)], (t, s + 1), mine & has_dn, mine & has_up),
            remote(a.at[pl.ds(0, TILE)], st.at[b, pl.ds(6 * TILE, TILE)], (t, s - 1), mine & has_up, mine & has_dn),
        ]
    start(near)
    start(fields)
    start(far)

    def staged(q, tile, r8, h):
        return st[q, pl.ds(tile * TILE + r8 + 8 * h, 8, stride=16), :]

    def coefficients(tile_lo, tiles):
        def body(i, _):
            tile = tile_lo + i
            for r8 in range(8):
                row = tile * 8 + r8
                for h in range(2):
                    d, b, c, k, sr = [staged(q, tile, r8, h) for q in range(5)]
                    u = d + jnp.maximum(b, 0.0)
                    n = d - jnp.minimum(b, 0.0)
                    le = d + jnp.maximum(c, 0.0)
                    ri = d - jnp.minimum(c, 0.0)
                    a = k - ((u + n) + (le + ri))
                    co[0, row, h] = 1.0 + a
                    co[1, row, h] = k
                    co[2, row, h] = u
                    co[3, row, h] = n
                    co[4, row, h] = le
                    co[5, row, h] = ri
                    co[6, row, h] = sr
            return 0

        lax.fori_loop(0, tiles, body, 0)

    def coarse_coefficients():
        def body(i, _):
            for j in range(4):
                row = OFF - 4 + i * 4 + j
                for h in range(2):
                    k, u, n, le, ri, sr = [8.0 * co[q, row, h] for q in range(1, 7)]
                    cc[0, row, h] = 1.0 + (k - ((u + n) + (le + ri)))
                    for q, x in enumerate((k, u, n, le, ri, sr)):
                        cc[1 + q, row, h] = x
            return 0

        lax.fori_loop(0, 10, body, 0)

    def field(q, dest, tile_lo, tiles):
        def body(i, _):
            tile = tile_lo + i
            for r8 in range(8):
                for h in range(2):
                    ping[dest, tile * 8 + r8, h] = staged(q, tile, r8, h)
            return 0

        lax.fori_loop(0, tiles, body, 0)

    def sides(a, b):
        ra, rb = pltpu.roll(a, 1, 1), pltpu.roll(b, 1, 1)
        la = jnp.where(first_lane, pltpu.roll(rb, 1, 0), ra)
        lb = jnp.where(first_lane, ra, rb)
        qa, qb = pltpu.roll(a, 127, 1), pltpu.roll(b, 127, 1)
        ga = jnp.where(last_lane, qb, qa)
        gb = jnp.where(last_lane, pltpu.roll(qa, 7, 0), qb)
        return (la, lb), (ga, gb)

    def step(state, coef, base, n, emit):
        load = lambda row: [state[row, h] for h in range(2)]
        up, ce = load(base - 1), load(base)
        for r in range(n):
            row = base + r
            dn = load(row + 1)
            left, right = sides(*ce)
            for h in range(2):
                a, k, u, d, le, ri, sr = [coef[q, row, h] for q in range(7)]
                x = ce[h]
                y = x * (a - k * (x * x)) + sr
                y = y + u * up[h] + d * dn[h]
                y = y + le * left[h] + ri * right[h]
                emit(r, row, h, y, x)
            up, ce = ce, dn

    for i, (cond, a, b) in enumerate(loads):
        when(cond, lambda a=a, b=b, i=i: pltpu.make_async_copy(a, b, lsem.at[i]).wait())
    coefficients(2, 4)
    field(5, 0, 2, 4)
    field(6, 1, 2, 4)
    wait_recv(near)
    start(near_on)
    wait_recv(fields)
    for q in range(2):
        field(5 + q, q, 1, 1)
        field(5 + q, q, 6, 1)
    wait_recv(near_on)
    coefficients(1, 1)
    coefficients(6, 1)

    def edge(f, side):
        from_row, to_row = ((OFF + MAIN - HALO, OFF - HALO), (OFF, OFF + MAIN))[side]
        return pltpu.make_async_remote_copy(
            src_ref=again_in.at[f, pl.ds(from_row, HALO)], dst_ref=again_in.at[f, pl.ds(to_row, HALO)],
            send_sem=esend.at[2 * f + side], recv_sem=erecv.at[2 * f + side],
            device_id=(t, s + 1 - 2 * side), device_id_type=MESH,
        )

    n_fields = jnp.where(origin, 1, 2)

    def keep(dest, f):
        def emit(r, row, h, y, x):
            dest[f, row, h] = y

        return emit

    def relax(f, _):
        def two(k, _):
            step(ping.at[f], co, OFF - 7, 46, keep(pong, f))
            step(pong.at[f], co, OFF - 6, 44, keep(ping, f))
            return 0

        lax.fori_loop(0, 3, two, 0)
        step(ping.at[f], co, OFF - 1, 34, keep(pong, f))
        step(pong.at[f], co, OFF, MAIN, keep(again_in, f))
        pl.when(has_dn)(lambda: edge(f, 0).start())
        pl.when(has_up)(lambda: edge(f, 1).start())
        return 0

    lax.fori_loop(0, n_fields, relax, 0)

    def first_copy(m):
        rows = pl.ds(chunk_row(m), 4)
        return pltpu.make_async_remote_copy(
            src_ref=again_in.at[0, rows], dst_ref=prev.at[rows], send_sem=fsend.at[m], recv_sem=frecv.at[m],
            device_id=(0, s), device_id_type=MESH,
        )

    def chunk_row(m):
        return OFF + jnp.where(odd, 4 * m, 28 - 4 * m)

    def each_chunk(body):
        def one(m, _):
            body(m)
            return 0

        lax.fori_loop(0, 8, one, 0)

    pl.when(origin)(lambda: each_chunk(lambda m: first_copy(m).start()))
    wait_recv(far)
    start(far_on)
    wait_recv(far_on)
    coefficients(0, 1)
    coefficients(7, 1)
    coarse_coefficients()

    def again(f, _):
        pl.when(has_up)(lambda: edge(f, 0).wait_recv())
        pl.when(has_dn)(lambda: edge(f, 1).wait_recv())

        def emit_first(r, row, h, y, x):
            ping[f, row, h] = y
            if 7 <= r < 47:
                first_coarse[f, row, h] = 8.0 * y - 7.0 * x

        step(again_in.at[f], co, OFF - 11, 54, emit_first)

        def two(k, _):
            step(ping.at[f], co, OFF - 10, 52, keep(pong, f))
            step(pong.at[f], co, OFF - 9, 50, keep(ping, f))
            return 0

        lax.fori_loop(0, 3, two, 0)

        def emit_last(r, row, h, y, x):
            pong[f, row, h] = y
            fc[2 * core + f, row, h] = y - first_coarse[f, row, h]

        step(ping.at[f], co, OFF - 4, 40, emit_last)
        return 0

    lax.fori_loop(0, n_fields, again, 0)

    give_f = [
        remote(fc.at[pl.ds(2, 2), pl.ds(OFF - 4, 40)], fc.at[pl.ds(2, 2), pl.ds(OFF - 4, 40)], (t - 1, s), (core == 1) & (z < z_last), (core == 0) & (z < z_last)),
    ]
    start(give_f)

    def main_copy(m):
        rows = pl.ds(chunk_row(m), 4)
        return pltpu.make_async_remote_copy(
            src_ref=v.at[4, rows], dst_ref=v.at[0, rows], send_sem=csend.at[m], recv_sem=crecv.at[m],
            device_id=(t + 2, s), device_id_type=MESH,
        )

    def edge_copy(i, from_row, to_row, ds):
        return pltpu.make_async_remote_copy(
            src_ref=v.at[4, pl.ds(from_row, 4)], dst_ref=v.at[0, pl.ds(to_row, 4)],
            send_sem=csend.at[8 + i], recv_sem=crecv.at[8 + i],
            device_id=(t + 2, s + ds), device_id_type=MESH,
        )

    low_from, low_to = OFF, OFF + MAIN
    top_from, top_to = OFF + MAIN - 4, OFF - 4

    def origin_copy(at, i):
        rows = pl.ds(at, 4)
        return pltpu.make_async_remote_copy(
            src_ref=pong.at[0, rows], dst_ref=v.at[0, rows], send_sem=csend.at[i], recv_sem=crecv.at[i],
            device_id=(0, s), device_id_type=MESH,
        )

    end_edge = jnp.where(odd, has_dn, has_up)
    start_edge = OFF + jnp.where(odd, -4, MAIN)
    end_edge_row = OFF + jnp.where(odd, MAIN, -4)

    @pl.when(origin)
    def _():
        origin_copy(start_edge, 8).start()
        each_chunk(lambda m: origin_copy(chunk_row(m), m).start())
        pl.when(end_edge)(lambda: origin_copy(end_edge_row, 9).start())

    def give_copy(m):
        rows = pl.ds(chunk_row(m), 4)
        return pltpu.make_async_remote_copy(
            src_ref=v.at[pl.ds(1, 3), rows], dst_ref=v.at[pl.ds(1, 3), rows],
            send_sem=xsend.at[m], recv_sem=xrecv.at[m], device_id=(t + 1, s), device_id_type=MESH,
        )

    def onward_copy(m):
        rows = pl.ds(chunk_row(m), 4)
        return pltpu.make_async_remote_copy(
            src_ref=v.at[3, rows], dst_ref=prev.at[rows], send_sem=fsend.at[m], recv_sem=frecv.at[m],
            device_id=(t + 1, s), device_id_type=MESH,
        )

    def to_out(state, o, row):
        tile = (row - OFF) // 8
        r8 = (row - OFF) % 8
        for h in range(2):
            obuf[o, pl.ds(tile * TILE + r8 + 8 * h, 8, stride=16), :] = state[row, h]

    def send_edges(m):
        pl.when((m == 0) & odd)(lambda: edge_copy(0, low_from, low_to, -1).start())
        pl.when((m == 0) & jnp.logical_not(odd))(lambda: edge_copy(0, top_from, top_to, 1).start())
        pl.when((m == 7) & odd & has_dn)(lambda: edge_copy(1, top_from, top_to, 1).start())
        pl.when((m == 7) & jnp.logical_not(odd) & has_up)(lambda: edge_copy(1, low_from, low_to, -1).start())

    def chain():
        wait_recv(give_f)

        def level(k, base, n):
            def emit(r, row, h, y, x):
                v[k, row, h] = y + fc[k - 1, row, h]

            step(v.at[k - 1], cc, base, n, emit)

        def base_of(i, k):
            return OFF + jnp.where(odd, 4 * i - 4 - k, 32 - 4 * i + k)

        def turn(i, _):
            pl.when(i == 1)(lambda: edge_copy(0, low_from, low_to, 0).wait_recv())
            pl.when(i < 9)(lambda: main_copy(jnp.minimum(i - 1, 7)).wait_recv())
            pl.when((i == 9) & end_edge)(lambda: edge_copy(1, low_from, low_to, 0).wait_recv())
            pl.when(i == 1)(lambda: level(1, base_of(0, 1), 4))
            level(1, base_of(i, 1), 4)
            level(2, base_of(i, 2), 4)
            m = i - 2

            @pl.when(z < z_last)
            def _():
                level(3, base_of(i, 3), 4)

                @pl.when(i > 1)
                def _():
                    level(4, base_of(i, 4), 4)
                    send_edges(m)
                    main_copy(m).start()

            pl.when(i > 1)(lambda: give_copy(m).start())
            return 0

        lax.fori_loop(1, 10, turn, 0)

    def finish_first():
        def body(m):
            onward_copy(m).wait_recv()
            for j in range(4):
                to_out(prev, 0, chunk_row(m) + j)
                to_out(v.at[0], 1, chunk_row(m) + j)

        each_chunk(body)

    def finish_second():
        def body(m):
            give_copy(m).wait_recv()
            pl.when(z < z_last)(lambda: onward_copy(m).start())
            for j in range(4):
                to_out(v.at[1], 0, chunk_row(m) + j)
                to_out(v.at[2], 1, chunk_row(m) + j)

        each_chunk(body)

    @pl.when(core == 0)
    def _():
        chain()
        finish_first()

    pl.when(core == 1)(finish_second)
    done = pltpu.make_async_copy(obuf, out, lsem.at[0])
    done.start()

    wait_send(near + far + near_on + far_on + fields + give_f)

    def edges_left(f, _):
        pl.when(has_dn)(lambda: edge(f, 0).wait_send())
        pl.when(has_up)(lambda: edge(f, 1).wait_send())
        return 0

    lax.fori_loop(0, n_fields, edges_left, 0)

    @pl.when(core == 0)
    def _():
        def drain(m):
            pl.when(z < z_last)(lambda: main_copy(m).wait_send())
            give_copy(m).wait_send()

        each_chunk(drain)
        pl.when(z < z_last)(lambda: edge_copy(0, low_from, low_to, 0).wait_send())
        pl.when((z < z_last) & end_edge)(lambda: edge_copy(1, low_from, low_to, 0).wait_send())

    pl.when((core == 1) & (z < z_last))(lambda: each_chunk(lambda m: onward_copy(m).wait_send()))

    @pl.when(origin)
    def _():
        def drain(m):
            first_copy(m).wait_send()
            origin_copy(chunk_row(m), m).wait_send()

        each_chunk(drain)
        origin_copy(start_edge, 8).wait_send()
        pl.when(end_edge)(lambda: origin_copy(end_edge_row, 9).wait_send())

    done.wait()


def tiles(x):
    lead = x.shape[:-2]
    n = len(lead)
    y = x.reshape(lead + (4, 8, 16, 128))
    y = y.transpose(tuple(range(n)) + (n, n + 2, n + 1, n + 3))
    return y.reshape(lead + (512, 128))


def shards(coarse_guess, initial, diffusion, velocity, reaction, source):
    hbm = pl.BlockSpec(memory_space=pl.ANY)
    state = (2, 8, 128)
    out = pl.pallas_call(
        kernel,
        out_shape=jax.ShapeDtypeStruct((2, 512, 128), F32),
        in_specs=[hbm] * 6,
        out_specs=hbm,
        scratch_shapes=[
            pltpu.VMEM((7, 8 * TILE, 128), F32),
            pltpu.VMEM((7, ROWS) + state, F32),
            pltpu.VMEM((7, ROWS) + state, F32),
            pltpu.VMEM((2, ROWS) + state, F32),
            pltpu.VMEM((2, ROWS) + state, F32),
            pltpu.VMEM((2, ROWS) + state, F32),
            pltpu.VMEM((2, ROWS) + state, F32),
            pltpu.VMEM((4, ROWS) + state, F32),
            pltpu.VMEM((5, ROWS) + state, F32),
            pltpu.VMEM((ROWS,) + state, F32),
            pltpu.VMEM((2, 512, 128), F32),
            pltpu.SemaphoreType.DMA((8,)),
            pltpu.SemaphoreType.DMA((NSEM,)),
            pltpu.SemaphoreType.DMA((NSEM,)),
            pltpu.SemaphoreType.DMA((4,)),
            pltpu.SemaphoreType.DMA((4,)),
            pltpu.SemaphoreType.DMA((10,)),
            pltpu.SemaphoreType.DMA((10,)),
            pltpu.SemaphoreType.DMA((8,)),
            pltpu.SemaphoreType.DMA((8,)),
            pltpu.SemaphoreType.DMA((8,)),
            pltpu.SemaphoreType.DMA((8,)),
        ],
        compiler_params=pltpu.CompilerParams(
            collective_id=0, has_side_effects=True, vmem_limit_bytes=63 * 2**20
        ),
    )(tiles(coarse_guess), tiles(initial), tiles(diffusion), tiles(velocity), tiles(reaction), tiles(source))
    out = out.reshape(2, 4, 16, 8, 128).transpose(0, 1, 3, 2, 4)
    return out.reshape(2, 32, 2048)


def solution(mesh):
    return jax.shard_map(
        shards,
        mesh=mesh,
        in_specs=(
            P("tm", "space", None),
            P("space", None),
            P("space", None),
            P(None, "space", None),
            P("space", None),
            P("space", None),
        ),
        out_specs=P("tm", "space", None),
        check_vma=False,
    )
```

time: 126 us -> 70.6 us (0.56)
  Pallas kernels: 119 us -> 68.5 us
  local copies, waits for them, and re-layouts: 6.68 us -> 1.87 us
    pallas_call x1, Pallas kernels: 119 us -> 68.5 us  [shards(): pl.pallas_call(kernel, out_shape=jax.ShapeDtypeStruct((2, 512, 128), F32)...]
    unnamed x13 -> x1, local copies, waits for them, and re-layouts: 6.68 us -> 1.87 us
where the time goes in v2:
time: 70.6 us; the launch traced here: 70.4 us
  Pallas kernels  68.5 us (97%)
  local copies, waits for them, and re-layouts  1.87 us (3%)
    pallas_call x1, Pallas kernels, shards(): pl.pallas_call(kernel, out_shape=jax.ShapeDtypeStruct((2, 512, 128), F32)...  68.5 us
    unnamed x1, local copies, waits for them, and re-layouts  1.87 us

profile of v2, /device:TPU:249, one launch (start us, length us, event | category | flops | bytes accessed | tf_op | source)
XLA Modules:
  0.0 70.4 jit_solution(3964160622916787512)
XLA Ops:
  0.0 68.5 %shard_map.64 = f32[2,512,128]{2,1,0:T(8,128)} custom-call(f32[2,512,128]{2,1,0:T(8,128)} %bitcast.36, f32[512,128]{1,0:T(8,128)} %bitcast.38, f32[512,128]{1,0:T(8,128)} %bitcast.39, f32[2,512,128]{2,1,0:T(8,128)} %bitcast.37, f32[512,128]{1,0:T(8,128)} %bitcast.40, f32[512,128]{1,0:T(8,128)} %bitcast.41), custom_call_target="tpu_custom_call" | custom-call | tf_op jit(solution)/shard_map/pallas_call | solution.py:505
  68.6 1.9 %copy.8 = f32[2,32,2048]{2,1,0:T(8,128)} copy(f32[2,32,2048]{2,1,0:T(8,128)} %bitcast.35) | data formatting | bytes 1048576

commit v3 on v2

v3 whole, which is shorter than its diff:
```python
import functools

import jax
import jax.numpy as jnp
from jax import lax
from jax.experimental import pallas as pl
from jax.experimental.pallas import tpu as pltpu
from jax.sharding import PartitionSpec as P

MESH = pl.DeviceIdType.MESH
F32 = jnp.float32

OFF = 16
ROWS = 64
MAIN = 32
COARSEN = 8
HALO = 12
TILE = 128


NSEM = 64


def kernel(
    cg, init, dif, vel, rea, src,
    out,
    st, co, cc, edges_in, fc, fcx, v, prev,
    lsem, ssem, rsem, esend, erecv, csend, crecv, xsend, xrecv, fsend, frecv, isend, irecv,
    *lev,
):
    t = lax.axis_index("tm")
    s = lax.axis_index("space")
    t_last, s_last = lax.axis_size("tm") - 1, lax.axis_size("space") - 1
    z_last = t_last // 2
    z, core = t // 2, t % 2
    odd = s % 2 == 1
    has_up, has_dn = s > 0, s < s_last
    double = z >= 5
    single = z < 5
    exports = (z >= 4) & (z < z_last)
    lead = z < z_last - 1
    skips = lead & (z >= 3)
    forks = z == 3
    passes = z <= 3
    origin = t == t_last

    lane = lax.broadcasted_iota(jnp.int32, (8, 128), 1)
    first_lane, last_lane = lane == 0, lane == 127

    loads = [
        (None, dif, st.at[0, pl.ds(2 * TILE, 512)]),
        (None, vel, st.at[pl.ds(1, 2), pl.ds(2 * TILE, 512)]),
        (None, rea, st.at[3, pl.ds(2 * TILE, 512)]),
        (None, src, st.at[4, pl.ds(2 * TILE, 512)]),
        (t < t_last, cg.at[0], st.at[5, pl.ds(2 * TILE, 512)]),
        (t < t_last, cg.at[1], st.at[6, pl.ds(2 * TILE, 512)]),
        (origin, init, st.at[5, pl.ds(2 * TILE, 512)]),
    ]

    def when(cond, body):
        if cond is None:
            body()
        else:
            pl.when(cond)(body)

    for i, (cond, a, b) in enumerate(loads):
        when(cond, lambda a=a, b=b, i=i: pltpu.make_async_copy(a, b, lsem.at[i]).start())

    zero = jnp.zeros((8, 128), F32)

    def clear(at_stage, rows):
        def body(i, _):
            for q in range(7):
                st[q, pl.ds(at_stage + i * 8, 8), :] = zero
            return 0

        lax.fori_loop(0, 32, body, 0)

        def rows_body(i, _):
            for f in range(2):
                for h in range(2):
                    edges_in[f, (0 if rows < 0 else HALO) + i, h] = zero
            for h in range(2):
                v[0, OFF + rows + i, h] = zero
                for q in range(4):
                    fcx[q, OFF + rows + i, h] = zero
            return 0

        lax.fori_loop(0, HALO, rows_body, 0)

    pl.when(s == 0)(lambda: clear(0, -HALO))
    pl.when(s == s_last)(lambda: clear(6 * TILE, MAIN))

    partners = []

    def partner(ok, pt, ps):
        partners.append((ok & (ps >= 0) & (ps <= s_last), pt, ps))

    for ds in (-1, 1):
        partner(t >= 0, t, s + ds)
    for ds in (-1, 0, 1):
        partner((core == 0) & (z > 0), t - 2, s + ds)
        partner((core == 0) & (z < z_last), t + 2, s + ds)
        partner((core == 0) & skips, t + 4, s + ds)
        partner((core == 0) & double, t - 4, s + ds)
    for ds in (-1, 1):
        partner((core == 1) & exports, t + 1, s + ds)
        partner((core == 0) & double, t - 1, s + ds)
    partner(t > 0, t - 1, s)
    partner(t < t_last, t + 1, s)
    partner((t == 0) | origin, t_last - t, s)
    barrier = pltpu.get_barrier_semaphore()
    count = 0
    for ok, pt, ps in partners:
        @pl.when(ok)
        def _(pt=pt, ps=ps):
            pl.semaphore_signal(barrier, inc=1, device_id=(pt, ps), device_id_type=MESH)
        count = count + ok.astype(jnp.int32)

    pl.semaphore_wait(barrier, count)

    used = [0]

    def remote(source, dest, device, sends, receives):
        i = used[0]
        used[0] += 1
        cp = pltpu.make_async_remote_copy(
            src_ref=source, dst_ref=dest, send_sem=ssem.at[i], recv_sem=rsem.at[i],
            device_id=device, device_id_type=MESH,
        )
        return sends, receives, cp

    def start(copies):
        for sends, _, cp in copies:
            pl.when(sends)(lambda cp=cp: cp.start())

    def wait_recv(copies):
        for _, receives, cp in copies:
            pl.when(receives)(lambda cp=cp: cp.wait_recv())

    def wait_send(copies):
        for sends, _, cp in copies:
            pl.when(sends)(lambda cp=cp: cp.wait_send())

    near, far, near_on, far_on = [], [], [], []
    half = pl.multiple_of(core * (TILE // 2), TILE // 2)
    sibling = (t + 1 - 2 * core, s)
    for group, onward, up_from, up_to, dn_from, dn_to in (
        (near, near_on, 3 * TILE, 1 * TILE, 0, 6 * TILE),
        (far, far_on, 2 * TILE, 0, TILE, 7 * TILE),
    ):
        for a, b in ((dif, 0), (vel, None), (rea, 3), (src, 4)):
            def part(at, a=a):
                rows = pl.ds(at + half, TILE // 2)
                return a.at[:, rows] if len(a.shape) == 3 else a.at[rows]

            def stage(at, b=b):
                rows = pl.ds(at + half, TILE // 2)
                return st.at[pl.ds(1, 2), rows] if b is None else st.at[b, rows]

            group.append(remote(part(up_from), stage(up_to), (t, s + 1), has_dn, has_up))
            group.append(remote(part(dn_from), stage(dn_to), (t, s - 1), has_up, has_dn))
            onward.append(remote(stage(up_to), stage(up_to), sibling, has_up, has_up))
            onward.append(remote(stage(dn_to), stage(dn_to), sibling, has_dn, has_dn))
    fields = []
    for a, b, mine in ((cg.at[0], 5, t < t_last), (cg.at[1], 6, t < t_last), (init, 5, origin)):
        fields += [
            remote(a.at[pl.ds(3 * TILE, TILE)], st.at[b, pl.ds(TILE, TILE)], (t, s + 1), mine & has_dn, mine & has_up),
            remote(a.at[pl.ds(0, TILE)], st.at[b, pl.ds(6 * TILE, TILE)], (t, s - 1), mine & has_up, mine & has_dn),
        ]
    start(near)
    start(fields)
    start(far)

    def staged(q, tile, r8, h):
        return st[q, pl.ds(tile * TILE + r8 + 8 * h, 8, stride=16), :]

    def coefficients(tile_lo, tiles):
        def body(i, _):
            tile = tile_lo + i
            for r8 in range(8):
                row = tile * 8 + r8
                for h in range(2):
                    d, b, c, k, sr = [staged(q, tile, r8, h) for q in range(5)]
                    u = d + jnp.maximum(b, 0.0)
                    n = d - jnp.minimum(b, 0.0)
                    le = d + jnp.maximum(c, 0.0)
                    ri = d - jnp.minimum(c, 0.0)
                    a = k - ((u + n) + (le + ri))
                    co[0, row, h] = 1.0 + a
                    co[1, row, h] = k
                    co[2, row, h] = u
                    co[3, row, h] = n
                    co[4, row, h] = le
                    co[5, row, h] = ri
                    co[6, row, h] = sr
            return 0

        lax.fori_loop(0, tiles, body, 0)

    def coarse_coefficients():
        def body(i, _):
            for j in range(4):
                row = OFF - 8 + i * 4 + j
                for h in range(2):
                    k, u, n, le, ri, sr = [8.0 * co[q, row, h] for q in range(1, 7)]
                    cc[0, row, h] = 1.0 + (k - ((u + n) + (le + ri)))
                    for q, x in enumerate((k, u, n, le, ri, sr)):
                        cc[1 + q, row, h] = x
            return 0

        lax.fori_loop(0, 12, body, 0)

    def field(q, dest, tile_lo, tiles):
        def body(i, _):
            tile = tile_lo + i
            for r8 in range(8):
                for h in range(2):
                    lev[0][dest, tile * 8 + r8, h] = staged(q, tile, r8, h)
            return 0

        lax.fori_loop(0, tiles, body, 0)

    def sides(a, b):
        ra, rb = pltpu.roll(a, 1, 1), pltpu.roll(b, 1, 1)
        la = jnp.where(first_lane, pltpu.roll(rb, 1, 0), ra)
        lb = jnp.where(first_lane, ra, rb)
        qa, qb = pltpu.roll(a, 127, 1), pltpu.roll(b, 127, 1)
        ga = jnp.where(last_lane, qb, qa)
        gb = jnp.where(last_lane, pltpu.roll(qa, 7, 0), qb)
        return (la, lb), (ga, gb)

    def step(state, coef, base, n, emit):
        load = lambda row: [state[row, h] for h in range(2)]
        up, ce = load(base - 1), load(base)
        for r in range(n):
            row = base + r
            dn = load(row + 1)
            left, right = sides(*ce)
            for h in range(2):
                a, k, u, d, le, ri, sr = [coef[q, row, h] for q in range(7)]
                x = ce[h]
                y = x * (a - k * (x * x)) + sr
                y = y + u * up[h] + d * dn[h]
                y = y + le * left[h] + ri * right[h]
                emit(r, row, h, y, x)
            up, ce = ce, dn

    for i, (cond, a, b) in enumerate(loads):
        when(cond, lambda a=a, b=b, i=i: pltpu.make_async_copy(a, b, lsem.at[i]).wait())
    coefficients(2, 4)
    field(5, 0, 2, 4)
    field(6, 1, 2, 4)

    def edge(f, side):
        from_row, to_row = ((OFF + MAIN - HALO, 0), (OFF, HALO))[side]
        return pltpu.make_async_remote_copy(
            src_ref=lev[0].at[f, pl.ds(from_row, HALO)], dst_ref=edges_in.at[f, pl.ds(to_row, HALO)],
            send_sem=esend.at[2 * f + side], recv_sem=erecv.at[2 * f + side],
            device_id=(t, s + 1 - 2 * side), device_id_type=MESH,
        )

    def chunk_row(m):
        return OFF + jnp.where(odd, 4 * m, 28 - 4 * m)

    def each_chunk(body):
        def one(m, _):
            body(m)
            return 0

        lax.fori_loop(0, 8, one, 0)

    def first_copy(m):
        rows = pl.ds(chunk_row(m), 4)
        return pltpu.make_async_remote_copy(
            src_ref=lev[0].at[0, rows], dst_ref=prev.at[rows], send_sem=fsend.at[m], recv_sem=frecv.at[m],
            device_id=(0, s), device_id_type=MESH,
        )

    n_fields = jnp.where(origin, 1, 2)

    def fine(f, k, base, n):
        def emit(r, row, h, y, x):
            lev[k][f, row, h] = y
            if k == COARSEN:
                fc[2 * core + f, row, h] = y - (8.0 * lev[1][f, row, h] - 7.0 * lev[0][f, row, h])

        step(lev[k - 1].at[f], co, base, n, emit)

    def interior(f, _):
        for k in range(1, COARSEN + 1):
            fine(f, k, OFF + k, MAIN - 2 * k)
        return 0

    def wedges(f, width):
        for k in range(1, COARSEN + 1):
            fine(f, k, OFF - width + k, width)
            fine(f, k, OFF + MAIN - k, width)

    def first_edges(f, _):
        wedges(f, COARSEN)
        for r in range(MAIN):
            for h in range(2):
                lev[0][f, OFF + r, h] = lev[COARSEN][f, OFF + r, h]
        pl.when(has_dn)(lambda: edge(f, 0).start())
        pl.when(has_up)(lambda: edge(f, 1).start())
        return 0

    def second_edges(f, _):
        pl.when(has_up)(lambda: edge(f, 0).wait_recv())
        pl.when(has_dn)(lambda: edge(f, 1).wait_recv())
        for r in range(HALO):
            for h in range(2):
                lev[0][f, OFF - HALO + r, h] = edges_in[f, r, h]
                lev[0][f, OFF + MAIN + r, h] = edges_in[f, HALO + r, h]
        wedges(f, HALO)
        return 0

    def relaxation(turn, _):
        lax.fori_loop(0, n_fields, interior, 0)

        @pl.when(turn == 0)
        def _():
            wait_recv(near)
            start(near_on)
            wait_recv(fields)
            for q in range(2):
                field(5 + q, q, 1, 1)
                field(5 + q, q, 6, 1)
            wait_recv(near_on)
            coefficients(1, 1)
            coefficients(6, 1)
            lax.fori_loop(0, n_fields, first_edges, 0)
            pl.when(origin)(lambda: each_chunk(lambda m: first_copy(m).start()))
            wait_recv(far)
            start(far_on)

        @pl.when(turn == 1)
        def _():
            wait_recv(far_on)
            coefficients(0, 1)
            coefficients(7, 1)
            coarse_coefficients()
            lax.fori_loop(0, n_fields, second_edges, 0)

        return 0

    lax.fori_loop(0, 2, relaxation, 0)

    give_f = [
        remote(fc.at[pl.ds(2, 2), pl.ds(OFF - 4, 40)], fc.at[pl.ds(2, 2), pl.ds(OFF - 4, 40)], (t - 1, s), (core == 1) & lead, (core == 0) & lead),
    ]
    start(give_f)

    def send_ahead(kind):
        from_row, to_row, n, ds = (
            (OFF - 4, OFF - 4, 40, 0), (OFF + MAIN - 8, OFF - 8, 4, 1), (OFF + 4, OFF + MAIN + 4, 4, -1),
        )[kind]
        fields = pl.ds(2 * core, 2)
        return pltpu.make_async_remote_copy(
            src_ref=fc.at[fields, pl.ds(from_row, n)], dst_ref=fcx.at[fields, pl.ds(to_row, n)],
            send_sem=isend.at[kind], recv_sem=irecv.at[3 * core + kind],
            device_id=(t + 2 - core, s + ds), device_id_type=MESH,
        )

    def arrive_ahead(c, kind):
        n = (40, 4, 4)[kind]
        rows = fcx.at[pl.ds(2 * c, 2), pl.ds(OFF - 4, n)]
        return pltpu.make_async_remote_copy(
            src_ref=rows, dst_ref=rows, send_sem=isend.at[kind], recv_sem=irecv.at[3 * c + kind],
            device_id=(t, s), device_id_type=MESH,
        )

    @pl.when(exports)
    def _():
        send_ahead(0).start()
        pl.when(has_dn)(lambda: send_ahead(1).start())
        pl.when(has_up)(lambda: send_ahead(2).start())

    def main_copy(top, hop, m, later=0):
        rows = pl.ds(chunk_row(m), 4)
        return pltpu.make_async_remote_copy(
            src_ref=v.at[top, rows], dst_ref=v.at[0, rows], send_sem=csend.at[later + m], recv_sem=crecv.at[m + 2],
            device_id=(t + 2 * hop, s), device_id_type=MESH,
        )

    inward = jnp.where(odd, -1, 1)

    def edge_copy(top, hop, m, later=0):
        there = jnp.where(m < 4, -1 - m, 15 - m)
        to_row = OFF + jnp.where(odd, 28 - 4 * there, 4 * there)
        return pltpu.make_async_remote_copy(
            src_ref=v.at[top, pl.ds(chunk_row(m), 4)], dst_ref=v.at[0, pl.ds(to_row, 4)],
            send_sem=csend.at[later + 8 + jnp.where(m < 4, m, m - 4)], recv_sem=crecv.at[there + 2],
            device_id=(t + 2 * hop, s + jnp.where(m < 4, inward, -inward)), device_id_type=MESH,
        )

    def arrived(slot):
        rows = v.at[0, pl.ds(OFF, 4)]
        return pltpu.make_async_remote_copy(
            src_ref=rows, dst_ref=rows, send_sem=csend.at[0], recv_sem=crecv.at[slot],
            device_id=(t, s), device_id_type=MESH,
        )

    def origin_copy(m):
        rows = pl.ds(chunk_row(m), 4)
        return pltpu.make_async_remote_copy(
            src_ref=lev[COARSEN].at[0, rows], dst_ref=v.at[0, rows], send_sem=csend.at[m + 2], recv_sem=crecv.at[m + 2],
            device_id=(0, s), device_id_type=MESH,
        )

    end_edge = jnp.where(odd, has_dn, has_up)

    @pl.when(origin)
    def _():
        origin_copy(-1).start()
        each_chunk(lambda m: origin_copy(m).start())
        pl.when(end_edge)(lambda: origin_copy(8).start())

    def give_copy(m, low=1):
        rows = pl.ds(chunk_row(m), 4)
        return pltpu.make_async_remote_copy(
            src_ref=v.at[pl.ds(low, 2), rows], dst_ref=v.at[pl.ds(1, 2), rows],
            send_sem=xsend.at[m], recv_sem=xrecv.at[m], device_id=(t + 1, s), device_id_type=MESH,
        )

    def onward_copy(m):
        rows = pl.ds(chunk_row(m), 4)
        return pltpu.make_async_remote_copy(
            src_ref=v.at[3, rows], dst_ref=prev.at[rows], send_sem=fsend.at[m], recv_sem=frecv.at[m],
            device_id=(t + 2, s), device_id_type=MESH,
        )

    def to_out(state, o, row):
        tile = (row - OFF) // 8
        r8 = (row - OFF) % 8
        for h in range(2):
            out[o, pl.ds(tile * TILE + r8 + 8 * h, 8, stride=16), :] = state[row, h]

    def state_out(top, hop, m, deep, act, later=0):
        at_start = (m == 0) | (deep & (m == 1))
        at_end = (m == 7) | (deep & (m == 6))
        pl.when(at_start | (at_end & end_edge))(lambda: act(edge_copy(top, hop, m, later)))
        act(main_copy(top, hop, m, later))

    def begin(copy):
        copy.start()

    def left(copy):
        copy.wait_send()

    no = t < 0
    hop = jnp.where(skips, 2, 1)

    def second_target(top, act):
        pl.when(forks)(lambda: each_chunk(lambda m: state_out(top, 1, m, no, act, 12)))

    def level(k, coarse_forcing, base, n):
        def emit(r, row, h, y, x):
            v[k, row, h] = y + coarse_forcing[row, h]

        step(v.at[k - 1], cc, base, n, emit)

    def chain_single():
        wait_recv(give_f)

        def base_of(i, k):
            return OFF + jnp.where(odd, 4 * i - 4 - k, 32 - 4 * i + k)

        def turn(i, _):
            pl.when(i == 1)(lambda: arrived(1).wait_recv())
            pl.when((i < 9) | end_edge)(lambda: arrived(i + 1).wait_recv())
            pl.when(i == 1)(lambda: level(1, fc.at[0], OFF + jnp.where(odd, -5, 29), 8))
            pl.when(i > 1)(lambda: level(1, fc.at[0], base_of(i, 1), 4))
            level(2, fc.at[1], base_of(i, 2), 4)
            m = i - 2

            @pl.when(lead)
            def _():
                level(3, fc.at[2], base_of(i, 3), 4)

                @pl.when(i > 1)
                def _():
                    level(4, fc.at[3], base_of(i, 4), 4)
                    state_out(4, hop, m, skips, begin)

            pl.when(i > 1)(lambda: give_copy(m).start())
            return 0

        lax.fori_loop(1, 10, turn, 0)
        second_target(4, begin)
        pl.when(passes)(lambda: each_chunk(lambda m: onward_copy(m).start()))

    def chain_double():
        for c in range(2):
            arrive_ahead(c, 0).wait_recv()
            pl.when(has_up)(lambda c=c: arrive_ahead(c, 1).wait_recv())
            pl.when(has_dn)(lambda c=c: arrive_ahead(c, 2).wait_recv())
        wait_recv(give_f)

        def one(j, k):
            level(k, fcx.at[k - 1] if k <= 4 else fc.at[k - 5], jnp.where(odd, 8 * j + (OFF - 8 - k), (OFF + 32 + k) - 8 * j), 8)

        def turn(j, _):
            for i in range(2):
                pl.when((j < 5) | end_edge)(lambda i=i: arrived(2 * j + i).wait_recv())
            for k in (1, 2, 3):
                one(j, k)

            @pl.when(j >= 1)
            def _():
                for k in (4, 5, 6):
                    one(j, k)

                @pl.when(lead)
                def _():
                    one(j, 7)
                    pl.when(j >= 2)(lambda: one(j, 8))

            @pl.when(j >= 2)
            def _():
                for i in range(2):
                    m = 2 * (j - 2) + i
                    pl.when(lead)(lambda m=m: state_out(8, hop, m, skips, begin))
                    give_copy(m, 5).start()

            return 0

        lax.fori_loop(0, 6, turn, 0)

    def finish_first():
        def body(m):
            onward_copy(m).wait_recv()
            for j in range(4):
                to_out(prev, 0, chunk_row(m) + j)
                to_out(v.at[0], 1, chunk_row(m) + j)

        each_chunk(body)

    def finish_double():
        def body(m):
            for j in range(4):
                to_out(v.at[3], 0, chunk_row(m) + j)
                to_out(v.at[4], 1, chunk_row(m) + j)

        each_chunk(body)

    def finish_second():
        def body(m):
            give_copy(m).wait_recv()
            for j in range(4):
                to_out(v.at[1], 0, chunk_row(m) + j)
                to_out(v.at[2], 1, chunk_row(m) + j)

        each_chunk(body)

    @pl.when((core == 0) & single)
    def _():
        chain_single()
        finish_first()

    @pl.when((core == 0) & double)
    def _():
        chain_double()
        finish_double()

    pl.when(core == 1)(finish_second)

    wait_send(near + far + near_on + far_on + fields + give_f)

    def edges_left(f, _):
        pl.when(has_dn)(lambda: edge(f, 0).wait_send())
        pl.when(has_up)(lambda: edge(f, 1).wait_send())
        return 0

    lax.fori_loop(0, n_fields, edges_left, 0)

    def drain(top, low):
        def body(m):
            pl.when(lead)(lambda: state_out(top, hop, m, skips, left))
            give_copy(m, low).wait_send()

        each_chunk(body)

    @pl.when((core == 0) & single)
    def _():
        drain(4, 1)
        second_target(4, left)
        pl.when(passes)(lambda: each_chunk(lambda m: onward_copy(m).wait_send()))

    pl.when((core == 0) & double)(lambda: drain(8, 5))

    @pl.when(exports)
    def _():
        send_ahead(0).wait_send()
        pl.when(has_dn)(lambda: send_ahead(1).wait_send())
        pl.when(has_up)(lambda: send_ahead(2).wait_send())

    @pl.when(origin)
    def _():
        def drain_origin(m):
            first_copy(m).wait_send()
            origin_copy(m).wait_send()

        each_chunk(drain_origin)
        origin_copy(-1).wait_send()
        pl.when(end_edge)(lambda: origin_copy(8).wait_send())


def tiles(x):
    lead = x.shape[:-2]
    n = len(lead)
    y = x.reshape(lead + (4, 8, 16, 128))
    y = y.transpose(tuple(range(n)) + (n, n + 2, n + 1, n + 3))
    return y.reshape(lead + (512, 128))


def shards(coarse_guess, initial, diffusion, velocity, reaction, source):
    hbm = pl.BlockSpec(memory_space=pltpu.HBM)
    state = (2, 8, 128)
    out = pl.pallas_call(
        kernel,
        out_shape=pltpu.VMEM((2, 512, 128), F32),
        in_specs=[hbm] * 6,
        out_specs=pl.BlockSpec(memory_space=pltpu.VMEM),
        scratch_shapes=[
            pltpu.VMEM((7, 8 * TILE, 128), F32),
            pltpu.VMEM((7, ROWS) + state, F32),
            pltpu.VMEM((7, ROWS) + state, F32),
            pltpu.VMEM((2, 2 * HALO) + state, F32),
            pltpu.VMEM((4, ROWS) + state, F32),
            pltpu.VMEM((4, ROWS) + state, F32),
            pltpu.VMEM((9, ROWS) + state, F32),
            pltpu.VMEM((ROWS,) + state, F32),
            pltpu.SemaphoreType.DMA((8,)),
            pltpu.SemaphoreType.DMA((NSEM,)),
            pltpu.SemaphoreType.DMA((NSEM,)),
            pltpu.SemaphoreType.DMA((4,)),
            pltpu.SemaphoreType.DMA((4,)),
            pltpu.SemaphoreType.DMA((24,)),
            pltpu.SemaphoreType.DMA((12,)),
            pltpu.SemaphoreType.DMA((8,)),
            pltpu.SemaphoreType.DMA((8,)),
            pltpu.SemaphoreType.DMA((8,)),
            pltpu.SemaphoreType.DMA((8,)),
            pltpu.SemaphoreType.DMA((3,)),
            pltpu.SemaphoreType.DMA((6,)),
        ] + [pltpu.VMEM((2, ROWS) + state, F32)] * (COARSEN + 1),
        compiler_params=pltpu.CompilerParams(
            collective_id=0, has_side_effects=True, vmem_limit_bytes=62 * 2**20
        ),
    )(tiles(coarse_guess), tiles(initial), tiles(diffusion), tiles(velocity), tiles(reaction), tiles(source))
    out = out.reshape(2, 4, 16, 8, 128).transpose(0, 1, 3, 2, 4)
    return out.reshape(2, 32, 2048)


def solution(mesh):
    return jax.shard_map(
        shards,
        mesh=mesh,
        in_specs=(
            P("tm", "space", None),
            P("space", None),
            P("space", None),
            P(None, "space", None),
            P("space", None),
            P("space", None),
        ),
        out_specs=P("tm", "space", None),
        check_vma=False,
    )
```

time: 70.6 us -> 63 us (0.89)
  Pallas kernels: 68.5 us -> 62.1 us
  local copies, waits for them, and re-layouts: 1.87 us -> 0.8 us
    pallas_call x1, Pallas kernels: 68.5 us -> 62.1 us  [shards(): pl.pallas_call(kernel, out_shape=pltpu.VMEM((2, 512, 128), F32), in_specs...]
    unnamed x1, local copies, waits for them, and re-layouts: 1.87 us -> 0.8 us
where the time goes in v3:
time: 63 us; the launch traced here: 62.9 us
  Pallas kernels  62.1 us (99%)
  local copies, waits for them, and re-layouts  0.8 us (1%)
    pallas_call x1, Pallas kernels, shards(): pl.pallas_call(kernel, out_shape=pltpu.VMEM((2, 512, 128), F32), in_specs...  62.1 us

profile of v3, /device:TPU:249, one launch (start us, length us, event | category | flops | bytes accessed | tf_op | source)
XLA Modules:
  0.0 62.9 jit_solution(5166102258371369110)
XLA Ops:
  0.0 62.1 %shard_map.64 = f32[2,512,128]{2,1,0:T(8,128)S(1)} custom-call(f32[2,512,128]{2,1,0:T(8,128)} %bitcast.36, f32[512,128]{1,0:T(8,128)} %bitcast.38, f32[512,128]{1,0:T(8,128)} %bitcast.39, f32[2,512,128]{2,1,0:T(8,128)} %bitcast.37, f32[512,128]{1,0:T(8,128)} %bitcast.40, f32[512,128]{1,0:T(8,128)} %bitcast.41), custom_call_target="tpu_custom_call" | custom-call | tf_op jit(solution)/shard_map/pallas_call | solution.py:621
  62.1 0.8 %copy.8 = f32[2,32,2048]{2,1,0:T(8,128)} copy(f32[2,32,2048]{2,1,0:T(8,128)S(1)} %bitcast.35) | data formatting | bytes 1048576

commit v4 on v3

--- a/solution.py
+++ b/solution.py
@@ -24,8 +24,8 @@
 def kernel(
     cg, init, dif, vel, rea, src,
     out,
-    st, co, cc, edges_in, fc, fcx, v, prev,
-    lsem, ssem, rsem, esend, erecv, csend, crecv, xsend, xrecv, fsend, frecv, isend, irecv,
+    st, co, cc, edges_in, fc, fcx, v,
+    lsem, ssem, rsem, esend, erecv, csend, crecv, xsend, xrecv, isend, irecv, gsend, grecv,
     *lev,
 ):
     t = lax.axis_index("tm")
@@ -41,8 +41,7 @@
     lead = z < z_last - 1
     skips = lead & (z >= 3)
     forks = z == 3
-    passes = z <= 3
-    origin = t == t_last
+    ends = t == t_last
 
     lane = lax.broadcasted_iota(jnp.int32, (8, 128), 1)
     first_lane, last_lane = lane == 0, lane == 127
@@ -52,9 +51,8 @@
         (None, vel, st.at[pl.ds(1, 2), pl.ds(2 * TILE, 512)]),
         (None, rea, st.at[3, pl.ds(2 * TILE, 512)]),
         (None, src, st.at[4, pl.ds(2 * TILE, 512)]),
-        (t < t_last, cg.at[0], st.at[5, pl.ds(2 * TILE, 512)]),
-        (t < t_last, cg.at[1], st.at[6, pl.ds(2 * TILE, 512)]),
-        (origin, init, st.at[5, pl.ds(2 * TILE, 512)]),
+        (t < t_last, cg.at[0], st.at[6, pl.ds(2 * TILE, 512)]),
+        (t == 0, init, st.at[5, pl.ds(2 * TILE, 512)]),
     ]
 
     def when(cond, body):
@@ -103,12 +101,8 @@
         partner((core == 0) & (z < z_last), t + 2, s + ds)
         partner((core == 0) & skips, t + 4, s + ds)
         partner((core == 0) & double, t - 4, s + ds)
-    for ds in (-1, 1):
-        partner((core == 1) & exports, t + 1, s + ds)
-        partner((core == 0) & double, t - 1, s + ds)
-    partner(t > 0, t - 1, s)
-    partner(t < t_last, t + 1, s)
-    partner((t == 0) | origin, t_last - t, s)
+        partner(t < t_last, t + 1, s + ds)
+        partner(t > 0, t - 1, s + ds)
     barrier = pltpu.get_barrier_semaphore()
     count = 0
     for ok, pt, ps in partners:
@@ -162,15 +156,20 @@
             group.append(remote(part(dn_from), stage(dn_to), (t, s - 1), has_up, has_dn))
             onward.append(remote(stage(up_to), stage(up_to), sibling, has_up, has_up))
             onward.append(remote(stage(dn_to), stage(dn_to), sibling, has_dn, has_dn))
-    fields = []
-    for a, b, mine in ((cg.at[0], 5, t < t_last), (cg.at[1], 6, t < t_last), (init, 5, origin)):
-        fields += [
-            remote(a.at[pl.ds(3 * TILE, TILE)], st.at[b, pl.ds(TILE, TILE)], (t, s + 1), mine & has_dn, mine & has_up),
-            remote(a.at[pl.ds(0, TILE)], st.at[b, pl.ds(6 * TILE, TILE)], (t, s - 1), mine & has_up, mine & has_dn),
-        ]
+    own = [
+        remote(cg.at[0, pl.ds(3 * TILE, TILE)], st.at[6, pl.ds(TILE, TILE)], (t, s + 1), (t < t_last) & has_dn, (t < t_last) & has_up),
+        remote(cg.at[0, pl.ds(0, TILE)], st.at[6, pl.ds(6 * TILE, TILE)], (t, s - 1), (t < t_last) & has_up, (t < t_last) & has_dn),
+    ]
+    shifted = [remote(cg.at[1], st.at[5, pl.ds(2 * TILE, 512)], (t + 1, s), t < t_last, t > 0)]
+    shifted_edges = [
+        remote(cg.at[1, pl.ds(3 * TILE, TILE)], st.at[5, pl.ds(TILE, TILE)], (t + 1, s + 1), (t < t_last) & has_dn, (t > 0) & has_up),
+        remote(cg.at[1, pl.ds(0, TILE)], st.at[5, pl.ds(6 * TILE, TILE)], (t + 1, s - 1), (t < t_last) & has_up, (t > 0) & has_dn),
+        remote(init.at[pl.ds(3 * TILE, TILE)], st.at[5, pl.ds(TILE, TILE)], (t, s + 1), (t == 0) & has_dn, (t == 0) & has_up),
+        remote(init.at[pl.ds(0, TILE)], st.at[5, pl.ds(6 * TILE, TILE)], (t, s - 1), (t == 0) & has_up, (t == 0) & has_dn),
+    ]
+    fields = shifted + own + shifted_edges
     start(near)
     start(fields)
-    start(far)
 
     def staged(q, tile, r8, h):
         return st[q, pl.ds(tile * TILE + r8 + 8 * h, 8, stride=16), :]
@@ -249,7 +248,6 @@
     for i, (cond, a, b) in enumerate(loads):
         when(cond, lambda a=a, b=b, i=i: pltpu.make_async_copy(a, b, lsem.at[i]).wait())
     coefficients(2, 4)
-    field(5, 0, 2, 4)
     field(6, 1, 2, 4)
 
     def edge(f, side):
@@ -270,14 +268,7 @@
 
         lax.fori_loop(0, 8, one, 0)
 
-    def first_copy(m):
-        rows = pl.ds(chunk_row(m), 4)
-        return pltpu.make_async_remote_copy(
-            src_ref=lev[0].at[0, rows], dst_ref=prev.at[rows], send_sem=fsend.at[m], recv_sem=frecv.at[m],
-            device_id=(0, s), device_id_type=MESH,
-        )
-
-    n_fields = jnp.where(origin, 1, 2)
+    n_fields = jnp.where(ends, 1, 2)
 
     def fine(f, k, base, n):
         def emit(r, row, h, y, x):
@@ -287,17 +278,33 @@
 
         step(lev[k - 1].at[f], co, base, n, emit)
 
-    def interior(f, _):
+    def interior(turn, i):
+        f = n_fields - 1 - i
+
+        @pl.when((turn == 0) & (f == 0))
+        def _():
+            wait_recv(shifted)
+            field(5, 0, 2, 4)
+
         for k in range(1, COARSEN + 1):
             fine(f, k, OFF + k, MAIN - 2 * k)
-        return 0
 
     def wedges(f, width):
         for k in range(1, COARSEN + 1):
             fine(f, k, OFF - width + k, width)
             fine(f, k, OFF + MAIN - k, width)
 
-    def first_edges(f, _):
+    def first_edges(i, _):
+        f = n_fields - 1 - i
+        pl.when(f == 0)(lambda: wait_recv(shifted_edges))
+        pl.when(f == 1)(lambda: wait_recv(own))
+        for q in range(2):
+
+            @pl.when(f == q)
+            def _(q=q):
+                field(5 + q, q, 1, 1)
+                field(5 + q, q, 6, 1)
+
         wedges(f, COARSEN)
         for r in range(MAIN):
             for h in range(2):
@@ -306,7 +313,48 @@
         pl.when(has_up)(lambda: edge(f, 1).start())
         return 0
 
-    def second_edges(f, _):
+    def send_ahead(kind, f):
+        from_row, to_row, n, ds = (
+            (OFF - 4, OFF - 4, 40, 0), (OFF + MAIN - 8, OFF - 8, 4, 1), (OFF + 4, OFF + MAIN + 4, 4, -1),
+        )[kind]
+        which = 2 * core + f
+        return pltpu.make_async_remote_copy(
+            src_ref=fc.at[which, pl.ds(from_row, n)], dst_ref=fcx.at[which, pl.ds(to_row, n)],
+            send_sem=isend.at[3 * f + kind], recv_sem=irecv.at[3 * which + kind],
+            device_id=(t + 2 - core, s + ds), device_id_type=MESH,
+        )
+
+    def arrive_ahead(which):
+        for kind, cond, n in ((0, None, 40), (1, has_up, 4), (2, has_dn, 4)):
+            rows = fcx.at[which, pl.ds(OFF - 4, n)]
+            copy = pltpu.make_async_remote_copy(
+                src_ref=rows, dst_ref=rows, send_sem=isend.at[kind], recv_sem=irecv.at[3 * which + kind],
+                device_id=(t, s), device_id_type=MESH,
+            )
+            when(cond, copy.wait_recv)
+
+    def ahead(f, act):
+        @pl.when(exports)
+        def _():
+            act(send_ahead(0, f))
+            pl.when(has_dn)(lambda: act(send_ahead(1, f)))
+            pl.when(has_up)(lambda: act(send_ahead(2, f)))
+
+    def give_forcing(f):
+        rows = fc.at[2 + f, pl.ds(OFF - 4, 40)]
+        return pltpu.make_async_remote_copy(
+            src_ref=rows, dst_ref=rows, send_sem=gsend.at[f], recv_sem=grecv.at[f],
+            device_id=(t - 1, s), device_id_type=MESH,
+        )
+
+    def begin(copy):
+        copy.start()
+
+    def left(copy):
+        copy.wait_send()
+
+    def second_edges(i, _):
+        f = n_fields - 1 - i
         pl.when(has_up)(lambda: edge(f, 0).wait_recv())
         pl.when(has_dn)(lambda: edge(f, 1).wait_recv())
         for r in range(HALO):
@@ -314,24 +362,26 @@
                 lev[0][f, OFF - HALO + r, h] = edges_in[f, r, h]
                 lev[0][f, OFF + MAIN + r, h] = edges_in[f, HALO + r, h]
         wedges(f, HALO)
+        pl.when(core == 1)(lambda: give_forcing(f).start())
+        ahead(f, begin)
         return 0
 
     def relaxation(turn, _):
-        lax.fori_loop(0, n_fields, interior, 0)
+        def inner(i, _):
+            interior(turn, i)
+            return 0
+
+        lax.fori_loop(0, n_fields, inner, 0)
 
         @pl.when(turn == 0)
         def _():
             wait_recv(near)
             start(near_on)
-            wait_recv(fields)
-            for q in range(2):
-                field(5 + q, q, 1, 1)
-                field(5 + q, q, 6, 1)
+            start(far)
             wait_recv(near_on)
             coefficients(1, 1)
             coefficients(6, 1)
             lax.fori_loop(0, n_fields, first_edges, 0)
-            pl.when(origin)(lambda: each_chunk(lambda m: first_copy(m).start()))
             wait_recv(far)
             start(far_on)
 
@@ -347,36 +397,6 @@
 
     lax.fori_loop(0, 2, relaxation, 0)
 
-    give_f = [
-        remote(fc.at[pl.ds(2, 2), pl.ds(OFF - 4, 40)], fc.at[pl.ds(2, 2), pl.ds(OFF - 4, 40)], (t - 1, s), (core == 1) & lead, (core == 0) & lead),
-    ]
-    start(give_f)
-
-    def send_ahead(kind):
-        from_row, to_row, n, ds = (
-            (OFF - 4, OFF - 4, 40, 0), (OFF + MAIN - 8, OFF - 8, 4, 1), (OFF + 4, OFF + MAIN + 4, 4, -1),
-        )[kind]
-        fields = pl.ds(2 * core, 2)
-        return pltpu.make_async_remote_copy(
-            src_ref=fc.at[fields, pl.ds(from_row, n)], dst_ref=fcx.at[fields, pl.ds(to_row, n)],
-            send_sem=isend.at[kind], recv_sem=irecv.at[3 * core + kind],
-            device_id=(t + 2 - core, s + ds), device_id_type=MESH,
-        )
-
-    def arrive_ahead(c, kind):
-        n = (40, 4, 4)[kind]
-        rows = fcx.at[pl.ds(2 * c, 2), pl.ds(OFF - 4, n)]
-        return pltpu.make_async_remote_copy(
-            src_ref=rows, dst_ref=rows, send_sem=isend.at[kind], recv_sem=irecv.at[3 * c + kind],
-            device_id=(t, s), device_id_type=MESH,
-        )
-
-    @pl.when(exports)
-    def _():
-        send_ahead(0).start()
-        pl.when(has_dn)(lambda: send_ahead(1).start())
-        pl.when(has_up)(lambda: send_ahead(2).start())
-
     def main_copy(top, hop, m, later=0):
         rows = pl.ds(chunk_row(m), 4)
         return pltpu.make_async_remote_copy(
@@ -402,33 +422,13 @@
             device_id=(t, s), device_id_type=MESH,
         )
 
-    def origin_copy(m):
-        rows = pl.ds(chunk_row(m), 4)
-        return pltpu.make_async_remote_copy(
-            src_ref=lev[COARSEN].at[0, rows], dst_ref=v.at[0, rows], send_sem=csend.at[m + 2], recv_sem=crecv.at[m + 2],
-            device_id=(0, s), device_id_type=MESH,
-        )
-
     end_edge = jnp.where(odd, has_dn, has_up)
 
-    @pl.when(origin)
-    def _():
-        origin_copy(-1).start()
-        each_chunk(lambda m: origin_copy(m).start())
-        pl.when(end_edge)(lambda: origin_copy(8).start())
-
-    def give_copy(m, low=1):
-        rows = pl.ds(chunk_row(m), 4)
+    def give_copy(low, j, n):
+        rows = pl.ds(OFF + jnp.where(odd, 8 * j, MAIN - n - 8 * j), n)
         return pltpu.make_async_remote_copy(
             src_ref=v.at[pl.ds(low, 2), rows], dst_ref=v.at[pl.ds(1, 2), rows],
-            send_sem=xsend.at[m], recv_sem=xrecv.at[m], device_id=(t + 1, s), device_id_type=MESH,
-        )
-
-    def onward_copy(m):
-        rows = pl.ds(chunk_row(m), 4)
-        return pltpu.make_async_remote_copy(
-            src_ref=v.at[3, rows], dst_ref=prev.at[rows], send_sem=fsend.at[m], recv_sem=frecv.at[m],
-            device_id=(t + 2, s), device_id_type=MESH,
+            send_sem=xsend.at[j], recv_sem=xrecv.at[j], device_id=(t + 1, s), device_id_type=MESH,
         )
 
     def to_out(state, o, row):
@@ -443,12 +443,6 @@
         pl.when(at_start | (at_end & end_edge))(lambda: act(edge_copy(top, hop, m, later)))
         act(main_copy(top, hop, m, later))
 
-    def begin(copy):
-        copy.start()
-
-    def left(copy):
-        copy.wait_send()
-
     no = t < 0
     hop = jnp.where(skips, 2, 1)
 
@@ -461,45 +455,58 @@
 
         step(v.at[k - 1], cc, base, n, emit)
 
+    def span(p, n, c=0):
+        return jnp.where(odd, p + (OFF + c), (OFF + MAIN - n - c) - p)
+
     def chain_single():
-        wait_recv(give_f)
-
-        def base_of(i, k):
-            return OFF + jnp.where(odd, 4 * i - 4 - k, 32 - 4 * i + k)
+        @pl.when(z == 0)
+        def _():
+            def body(i, _):
+                for j in range(4):
+                    row = OFF - 4 + 4 * i + j
+                    for h in range(2):
+                        v[0, row, h] = lev[0][0, row, h]
+                        v[1, row, h] = lev[COARSEN][0, row, h]
+                return 0
+
+            lax.fori_loop(0, 10, body, 0)
+
+        later = z > 0
 
         def turn(i, _):
-            pl.when(i == 1)(lambda: arrived(1).wait_recv())
-            pl.when((i < 9) | end_edge)(lambda: arrived(i + 1).wait_recv())
-            pl.when(i == 1)(lambda: level(1, fc.at[0], OFF + jnp.where(odd, -5, 29), 8))
-            pl.when(i > 1)(lambda: level(1, fc.at[0], base_of(i, 1), 4))
-            level(2, fc.at[1], base_of(i, 2), 4)
-            m = i - 2
-
-            @pl.when(lead)
+            pl.when(later & (i == 1))(lambda: arrived(1).wait_recv())
+            pl.when(later & ((i < 9) | end_edge))(lambda: arrived(i + 1).wait_recv())
+            pl.when(later & (i == 1))(lambda: level(1, fc.at[0], span(0, 8, -5), 8))
+            pl.when(later & (i > 1))(lambda: level(1, fc.at[0], span(4 * i, 4, -5), 4))
+            level(2, fc.at[1], span(4 * i, 4, -6), 4)
+
+            @pl.when(i == 1)
             def _():
-                level(3, fc.at[2], base_of(i, 3), 4)
-
-                @pl.when(i > 1)
-                def _():
-                    level(4, fc.at[3], base_of(i, 4), 4)
-                    state_out(4, hop, m, skips, begin)
-
-            pl.when(i > 1)(lambda: give_copy(m).start())
+                give_forcing(0).wait_recv()
+                give_forcing(1).wait_recv()
+
+            level(3, fc.at[2], span(4 * i, 4, -7), 4)
+
+            @pl.when(i > 1)
+            def _():
+                level(4, fc.at[3], span(4 * i, 4, -8), 4)
+                state_out(4, hop, i - 2, skips, begin)
+
             return 0
 
         lax.fori_loop(1, 10, turn, 0)
+        give_copy(2, 0, MAIN).start()
         second_target(4, begin)
-        pl.when(passes)(lambda: each_chunk(lambda m: onward_copy(m).start()))
 
     def chain_double():
-        for c in range(2):
-            arrive_ahead(c, 0).wait_recv()
-            pl.when(has_up)(lambda c=c: arrive_ahead(c, 1).wait_recv())
-            pl.when(has_dn)(lambda c=c: arrive_ahead(c, 2).wait_recv())
-        wait_recv(give_f)
-
         def one(j, k):
-            level(k, fcx.at[k - 1] if k <= 4 else fc.at[k - 5], jnp.where(odd, 8 * j + (OFF - 8 - k), (OFF + 32 + k) - 8 * j), 8)
+            coarse_forcing = fcx.at[k - 1] if k <= 4 else fc.at[k - 5]
+            level(k, coarse_forcing, span(8 * j, 8, -8 - k), 8)
+
+        for which in range(4):
+            arrive_ahead(which)
+        give_forcing(0).wait_recv()
+        pl.when(z < z_last)(lambda: give_forcing(1).wait_recv())
 
         def turn(j, _):
             for i in range(2):
@@ -509,64 +516,60 @@
 
             @pl.when(j >= 1)
             def _():
-                for k in (4, 5, 6):
+                for k in (4, 5, 6, 7):
                     one(j, k)
 
+            @pl.when(j >= 2)
+            def _():
                 @pl.when(lead)
                 def _():
-                    one(j, 7)
-                    pl.when(j >= 2)(lambda: one(j, 8))
-
-            @pl.when(j >= 2)
-            def _():
-                for i in range(2):
-                    m = 2 * (j - 2) + i
-                    pl.when(lead)(lambda m=m: state_out(8, hop, m, skips, begin))
-                    give_copy(m, 5).start()
+                    one(j, 8)
+                    for i in range(2):
+                        state_out(8, hop, 2 * (j - 2) + i, skips, begin)
+
+                give_copy(6, j - 2, 8).start()
 
             return 0
 
         lax.fori_loop(0, 6, turn, 0)
 
-    def finish_first():
-        def body(m):
-            onward_copy(m).wait_recv()
-            for j in range(4):
-                to_out(prev, 0, chunk_row(m) + j)
-                to_out(v.at[0], 1, chunk_row(m) + j)
-
-        each_chunk(body)
-
-    def finish_double():
-        def body(m):
-            for j in range(4):
-                to_out(v.at[3], 0, chunk_row(m) + j)
-                to_out(v.at[4], 1, chunk_row(m) + j)
-
-        each_chunk(body)
+    def finish_first(low):
+        def body(j, _):
+            for r in range(8):
+                row = OFF + 8 * j + r
+                to_out(v.at[low], 0, row)
+                to_out(v.at[low + 1], 1, row)
+            return 0
+
+        lax.fori_loop(0, 4, body, 0)
 
     def finish_second():
-        def body(m):
-            give_copy(m).wait_recv()
-            for j in range(4):
-                to_out(v.at[1], 0, chunk_row(m) + j)
-                to_out(v.at[2], 1, chunk_row(m) + j)
-
-        each_chunk(body)
+        def rows(first, n):
+            for r in range(n):
+                to_out(v.at[1], 0, first + r)
+                to_out(v.at[2], 1, first + r)
+
+        def body(j, _):
+            pl.when(double)(lambda: give_copy(6, j, 8).wait_recv())
+            rows(span(8 * j, 8), 8)
+            return 0
+
+        pl.when(single)(lambda: give_copy(2, 0, MAIN).wait_recv())
+        lax.fori_loop(0, 4, body, 0)
 
     @pl.when((core == 0) & single)
     def _():
         chain_single()
-        finish_first()
+        finish_first(0)
 
     @pl.when((core == 0) & double)
     def _():
         chain_double()
-        finish_double()
+        finish_first(4)
 
     pl.when(core == 1)(finish_second)
 
-    wait_send(near + far + near_on + far_on + fields + give_f)
+    wait_send(near + far + near_on + far_on + fields)
 
     def edges_left(f, _):
         pl.when(has_dn)(lambda: edge(f, 0).wait_send())
@@ -575,36 +578,31 @@
 
     lax.fori_loop(0, n_fields, edges_left, 0)
 
-    def drain(top, low):
+    def drain(top):
         def body(m):
             pl.when(lead)(lambda: state_out(top, hop, m, skips, left))
-            give_copy(m, low).wait_send()
 
         each_chunk(body)
 
     @pl.when((core == 0) & single)
     def _():
-        drain(4, 1)
+        drain(4)
+        give_copy(2, 0, MAIN).wait_send()
         second_target(4, left)
-        pl.when(passes)(lambda: each_chunk(lambda m: onward_copy(m).wait_send()))
-
-    pl.when((core == 0) & double)(lambda: drain(8, 5))
-
-    @pl.when(exports)
+
+    @pl.when((core == 0) & double)
     def _():
-        send_ahead(0).wait_send()
-        pl.when(has_dn)(lambda: send_ahead(1).wait_send())
-        pl.when(has_up)(lambda: send_ahead(2).wait_send())
-
-    @pl.when(origin)
-    def _():
-        def drain_origin(m):
-            first_copy(m).wait_send()
-            origin_copy(m).wait_send()
-
-        each_chunk(drain_origin)
-        origin_copy(-1).wait_send()
-        pl.when(end_edge)(lambda: origin_copy(8).wait_send())
+        drain(8)
+        for j in range(4):
+            give_copy(6, j, 8).wait_send()
+
+
+    def forcing_left(f, _):
+        pl.when(core == 1)(lambda: give_forcing(f).wait_send())
+        ahead(f, left)
+        return 0
+
+    lax.fori_loop(0, n_fields, forcing_left, 0)
 
 
 def tiles(x):
@@ -631,7 +629,6 @@
             pltpu.VMEM((4, ROWS) + state, F32),
             pltpu.VMEM((4, ROWS) + state, F32),
             pltpu.VMEM((9, ROWS) + state, F32),
-            pltpu.VMEM((ROWS,) + state, F32),
             pltpu.SemaphoreType.DMA((8,)),
             pltpu.SemaphoreType.DMA((NSEM,)),
             pltpu.SemaphoreType.DMA((NSEM,)),
@@ -641,10 +638,10 @@
             pltpu.SemaphoreType.DMA((12,)),
             pltpu.SemaphoreType.DMA((8,)),
             pltpu.SemaphoreType.DMA((8,)),
-            pltpu.SemaphoreType.DMA((8,)),
-            pltpu.SemaphoreType.DMA((8,)),
-            pltpu.SemaphoreType.DMA((3,)),
             pltpu.SemaphoreType.DMA((6,)),
+            pltpu.SemaphoreType.DMA((12,)),
+            pltpu.SemaphoreType.DMA((2,)),
+            pltpu.SemaphoreType.DMA((2,)),
         ] + [pltpu.VMEM((2, ROWS) + state, F32)] * (COARSEN + 1),
         compiler_params=pltpu.CompilerParams(
             collective_id=0, has_side_effects=True, vmem_limit_bytes=62 * 2**20

time: 63 us -> 60.6 us (0.962)
  Pallas kernels: 62.1 us -> 59.7 us
    pallas_call x1, Pallas kernels: 62.1 us -> 59.7 us  [shards(): pl.pallas_call(kernel, out_shape=pltpu.VMEM((2, 512, 128), F32), in_specs...]
where the time goes in v4:
time: 60.6 us; the launch traced here: 60.5 us
  Pallas kernels  59.7 us (99%)
  local copies, waits for them, and re-layouts  0.8 us (1%)
    pallas_call x1, Pallas kernels, shards(): pl.pallas_call(kernel, out_shape=pltpu.VMEM((2, 512, 128), F32), in_specs...  59.7 us

profile of v4, /device:TPU:249, one launch (start us, length us, event | category | flops | bytes accessed | tf_op | source)
XLA Modules:
  0.0 60.5 jit_solution(9247357188941693468)
XLA Ops:
  0.0 59.7 %shard_map.64 = f32[2,512,128]{2,1,0:T(8,128)S(1)} custom-call(f32[2,512,128]{2,1,0:T(8,128)} %bitcast.36, f32[512,128]{1,0:T(8,128)} %bitcast.38, f32[512,128]{1,0:T(8,128)} %bitcast.39, f32[2,512,128]{2,1,0:T(8,128)} %bitcast.37, f32[512,128]{1,0:T(8,128)} %bitcast.40, f32[512,128]{1,0:T(8,128)} %bitcast.41), custom_call_target="tpu_custom_call" | custom-call | tf_op jit(solution)/shard_map/pallas_call | solution.py:619
  59.7 0.8 %copy.8 = f32[2,32,2048]{2,1,0:T(8,128)} copy(f32[2,32,2048]{2,1,0:T(8,128)S(1)} %bitcast.35) | data formatting | bytes 1048576

commit v5 on v4

--- a/solution.py
+++ b/solution.py
@@ -278,6 +278,20 @@
 
         step(lev[k - 1].at[f], co, base, n, emit)
 
+    parts = (
+        (OFF - 4, OFF - 4, 12, 0), (OFF + 24, OFF + 24, 12, 0), (OFF + 8, OFF + 8, 16, 0),
+        (OFF + MAIN - 7, OFF - 7, 3, 1), (OFF + 4, OFF + MAIN + 4, 3, -1),
+    )
+
+    def send_ahead(part, f):
+        from_row, to_row, n, ds = parts[part]
+        which = 2 * core + f
+        return pltpu.make_async_remote_copy(
+            src_ref=fc.at[which, pl.ds(from_row, n)], dst_ref=fcx.at[which, pl.ds(to_row, n)],
+            send_sem=isend.at[5 * f + part], recv_sem=irecv.at[5 * which + part],
+            device_id=(t + 2 - core, s + ds), device_id_type=MESH,
+        )
+
     def interior(turn, i):
         f = n_fields - 1 - i
 
@@ -288,6 +302,7 @@
 
         for k in range(1, COARSEN + 1):
             fine(f, k, OFF + k, MAIN - 2 * k)
+        pl.when(exports & (turn == 1))(lambda: send_ahead(2, f).start())
 
     def wedges(f, width):
         for k in range(1, COARSEN + 1):
@@ -313,22 +328,12 @@
         pl.when(has_up)(lambda: edge(f, 1).start())
         return 0
 
-    def send_ahead(kind, f):
-        from_row, to_row, n, ds = (
-            (OFF - 4, OFF - 4, 40, 0), (OFF + MAIN - 8, OFF - 8, 4, 1), (OFF + 4, OFF + MAIN + 4, 4, -1),
-        )[kind]
-        which = 2 * core + f
-        return pltpu.make_async_remote_copy(
-            src_ref=fc.at[which, pl.ds(from_row, n)], dst_ref=fcx.at[which, pl.ds(to_row, n)],
-            send_sem=isend.at[3 * f + kind], recv_sem=irecv.at[3 * which + kind],
-            device_id=(t + 2 - core, s + ds), device_id_type=MESH,
-        )
-
     def arrive_ahead(which):
-        for kind, cond, n in ((0, None, 40), (1, has_up, 4), (2, has_dn, 4)):
-            rows = fcx.at[which, pl.ds(OFF - 4, n)]
+        conds = (None, None, None) + ((has_up, has_dn) if which < 3 else ())
+        for part, cond in enumerate(conds):
+            rows = fcx.at[which, pl.ds(OFF - 4, parts[part][2])]
             copy = pltpu.make_async_remote_copy(
-                src_ref=rows, dst_ref=rows, send_sem=isend.at[kind], recv_sem=irecv.at[3 * which + kind],
+                src_ref=rows, dst_ref=rows, send_sem=isend.at[part], recv_sem=irecv.at[5 * which + part],
                 device_id=(t, s), device_id_type=MESH,
             )
             when(cond, copy.wait_recv)
@@ -337,8 +342,10 @@
         @pl.when(exports)
         def _():
             act(send_ahead(0, f))
-            pl.when(has_dn)(lambda: act(send_ahead(1, f)))
-            pl.when(has_up)(lambda: act(send_ahead(2, f)))
+            act(send_ahead(1, f))
+            beyond = 2 * core + f < 3
+            pl.when(has_dn & beyond)(lambda: act(send_ahead(3, f)))
+            pl.when(has_up & beyond)(lambda: act(send_ahead(4, f)))
 
     def give_forcing(f):
         rows = fc.at[2 + f, pl.ds(OFF - 4, 40)]
@@ -600,6 +607,7 @@
     def forcing_left(f, _):
         pl.when(core == 1)(lambda: give_forcing(f).wait_send())
         ahead(f, left)
+        pl.when(exports)(lambda: send_ahead(2, f).wait_send())
         return 0
 
     lax.fori_loop(0, n_fields, forcing_left, 0)
@@ -638,8 +646,8 @@
             pltpu.SemaphoreType.DMA((12,)),
             pltpu.SemaphoreType.DMA((8,)),
             pltpu.SemaphoreType.DMA((8,)),
-            pltpu.SemaphoreType.DMA((6,)),
-            pltpu.SemaphoreType.DMA((12,)),
+            pltpu.SemaphoreType.DMA((10,)),
+            pltpu.SemaphoreType.DMA((20,)),
             pltpu.SemaphoreType.DMA((2,)),
             pltpu.SemaphoreType.DMA((2,)),
         ] + [pltpu.VMEM((2, ROWS) + state, F32)] * (COARSEN + 1),

time: 60.6 us -> 58.1 us (0.959)
  Pallas kernels: 59.7 us -> 57.2 us
    pallas_call x1, Pallas kernels: 59.7 us -> 57.2 us  [shards(): pl.pallas_call(kernel, out_shape=pltpu.VMEM((2, 512, 128), F32), in_specs...]
where the time goes in v5:
time: 58.1 us; the launch traced here: 58 us
  Pallas kernels  57.2 us (98%)
  local copies, waits for them, and re-layouts  0.8 us (1%)
    pallas_call x1, Pallas kernels, shards(): pl.pallas_call(kernel, out_shape=pltpu.VMEM((2, 512, 128), F32), in_specs...  57.2 us

profile of v5, /device:TPU:249, one launch (start us, length us, event | category | flops | bytes accessed | tf_op | source)
XLA Modules:
  0.0 58.0 jit_solution(15177968338486317760)
XLA Ops:
  0.0 57.2 %shard_map.64 = f32[2,512,128]{2,1,0:T(8,128)S(1)} custom-call(f32[2,512,128]{2,1,0:T(8,128)} %bitcast.36, f32[512,128]{1,0:T(8,128)} %bitcast.38, f32[512,128]{1,0:T(8,128)} %bitcast.39, f32[2,512,128]{2,1,0:T(8,128)} %bitcast.37, f32[512,128]{1,0:T(8,128)} %bitcast.40, f32[512,128]{1,0:T(8,128)} %bitcast.41), custom_call_target="tpu_custom_call" | custom-call | tf_op jit(solution)/shard_map/pallas_call | solution.py:627
  57.2 0.8 %copy.8 = f32[2,32,2048]{2,1,0:T(8,128)} copy(f32[2,32,2048]{2,1,0:T(8,128)S(1)} %bitcast.35) | data formatting | bytes 1048576
